TPU v7x, 32 devices: a whole 2x2x4 slice. The times are simulated.
32 devices in a mesh: dp: 8 (over y, x, core), tensor: 4 (over z).
Axes of the slice: x: 2, y: 2, z: 4, core: 2. Of those that a mesh axis runs over, the one named last changes fastest.
Arguments:
- stream: float32 [16384, 768], P(('dp', 'tensor')), may hold values from -6 to 6
- cotangent: float32 [16384, 768], P(('dp', 'tensor')), may hold values from -6 to 6
- gain_attention: float32 [768], replicated, may hold values from 0.5 to 1.5
- w_inputs: bfloat16 [3, 768, 768], P(None, None, 'tensor'), may hold values from -0.21875 to 0.21875
- w_output: bfloat16 [768, 768], P('tensor'), may hold values from -0.625 to 0.625
- gain_experts: float32 [768], replicated, may hold values from 0.5 to 1.5
- w_router: bfloat16 [768, 10], replicated, may hold values from -0.109375 to 0.109375
- w_carry: float32 [10, 10], replicated, may hold values from -2 to 2
- w_gate_up: bfloat16 [6, 768, 2, 2048], P(None, None, None, 'tensor'), may hold values from -0.21875 to 0.21875
- w_down: bfloat16 [6, 2048, 768], P(None, 'tensor'), may hold values from -0.1875 to 0.1875
- w_constant: float32 [2, 2, 768], replicated, may hold values from -0.21875 to 0.21875
- constant_vectors: float32 [2, 768], replicated, may hold values from -6 to 6
- previous_logits: float32 [16384, 10], P('dp'), may hold values from -3 to 3
- routes: int32 [16384, 2], P('dp'), may hold values from 0 to 9, all different within a row; in each aligned block of 2048 rows (0 to 2047, 2048 to 4095, ...) at most 768 rows name the same one
- valid: int32 [16384], P('dp'), may hold values from 0 to 1
- prefix: int32 [16], P('dp'), may hold values from 1 to 1024
Outputs:
- block_out: float32 [16384, 768], P(('dp', 'tensor'))
- grad_stream: float32 [16384, 768], P(('dp', 'tensor'))
- grad_gain_attention: float32 [768], replicated
- grad_inputs: float32 [3, 768, 768], P(None, None, 'tensor')
- grad_output: float32 [768, 768], P('tensor')
- grad_gain_experts: float32 [768], replicated
- grad_router: float32 [768, 10], replicated
- grad_carry: float32 [10, 10], replicated
- grad_gate_up: float32 [6, 768, 2, 2048], P(None, None, None, 'tensor')
- grad_down: float32 [6, 2048, 768], P(None, 'tensor')
- grad_constant: float32 [2, 2, 768], replicated
- grad_vectors: float32 [2, 768], replicated
- grad_previous: float32 [16384, 10], P(('dp', 'tensor'))
- rms_values: float32 [3], replicated
Inputs may be any that keep to these rules, and one draw needn't show every extreme that they name: `routes`: each row names two different experts: 0 to 5 feed-forward, 6 zero, 7 copy, the last two constant; among the rows of one index of dp no expert is named more than 768 times.
All inputs are finite; a program needn't handle non-finite values.
Results may differ from a plain program's by a relative error of at most 0.022.
Values may be sent and summed in bfloat16 or wider, within the bound.
No kernel may reach another device: no remote copies, remote signals or barrier semaphores. Data moves between devices by JAX's collectives and lax.ppermute only.
A program may use at most 192 MiB of HBM per device.

v0:
```python
import jax
import jax.numpy as jnp
from jax import lax
from jax.sharding import PartitionSpec as P

HEAD_DIM = 64
EXP_FFN = 6
SEQ_LEN = 1024
CAP = 768


EPSILON = 1e-05
HIGHEST = lax.Precision.HIGHEST


def norm_forward(values, gain):
    inverse = lax.rsqrt(jnp.mean(values * values, axis=-1, keepdims=True) + EPSILON)
    return (values * inverse * gain, inverse)


def norm_backward(values, inverse, gain, grad):
    scaled = grad * gain
    inner = jnp.mean(scaled * values, axis=-1, keepdims=True)
    return (
        inverse * scaled - values * inverse**3 * inner,
        jnp.sum(grad * values * inverse, axis=0),
    )


def tables(length):
    half = HEAD_DIM // 2
    frequency = 10000.0 ** (-jnp.arange(half, dtype=jnp.float32) / half)
    position = (jnp.arange(length, dtype=jnp.int32) % SEQ_LEN).astype(jnp.float32)
    angles = position[:, None] * frequency[None, :]
    return (jnp.cos(angles), jnp.sin(angles))


def rotate(values, cosine, sine):
    half = values.shape[-1] // 2
    first = values[..., :half]
    second = values[..., half:]
    cosine = cosine[:, None, :]
    sine = sine[:, None, :]
    return jnp.concatenate(
        [first * cosine - second * sine, first * sine + second * cosine], axis=-1
    )


def visible(start, rows, length, prefix_len, valid_rows):
    row = start + jnp.arange(rows, dtype=jnp.int32)[:, None]
    column = jnp.arange(length, dtype=jnp.int32)[None, :]
    return ((column <= row) | (column < prefix_len)) & ((valid_rows[None, :] > 0) | (column == row))


def block_scores(queries, keys, valid, prefix, first, block):
    begin = first // SEQ_LEN * SEQ_LEN
    query_rows = lax.dynamic_slice_in_dim(queries, first, block, 0)
    key_rows = lax.dynamic_slice_in_dim(keys, begin, SEQ_LEN, 0)
    valid_rows = lax.dynamic_slice_in_dim(valid, begin, SEQ_LEN, 0)
    allowed = visible(first - begin, block, SEQ_LEN, prefix[first // SEQ_LEN], valid_rows)
    scale = queries.shape[2] ** (-0.5)
    scores = (
        jnp.einsum("qhd,khd->hqk", query_rows, key_rows, preferred_element_type=jnp.float32) * scale
    )
    return (jnp.where(allowed[None], scores, -1e30), query_rows, key_rows, begin)


def attention_forward(queries, keys, values, valid, prefix):
    tokens, heads, width = queries.shape
    block = min(512, SEQ_LEN)

    def one_block(index):
        first = index * block
        scores, query_rows, key_rows, begin = block_scores(
            queries, keys, valid, prefix, first, block
        )
        value_rows = lax.dynamic_slice_in_dim(values, begin, SEQ_LEN, 0)
        top = jnp.max(scores, axis=-1, keepdims=True)
        weights = jnp.exp(scores - top)
        total = jnp.sum(weights, axis=-1, keepdims=True)
        shares = (weights / total).astype(jnp.bfloat16)
        mixed = jnp.einsum("hqk,khd->qhd", shares, value_rows, preferred_element_type=jnp.float32)
        return (mixed, jnp.transpose((top + jnp.log(total))[:, :, 0]))

    mixed, log_total = lax.map(one_block, jnp.arange(tokens // block, dtype=jnp.int32))
    return (mixed.reshape(tokens, heads, width), log_total.reshape(tokens, heads))


def attention_backward(queries, keys, values, valid, prefix, log_total, grad_mixed):
    tokens, heads, width = queries.shape
    block = min(512, SEQ_LEN)
    scale = width ** (-0.5)

    def one_block(carry, index):
        grad_keys, grad_values = carry
        first = index * block
        scores, query_rows, key_rows, begin = block_scores(
            queries, keys, valid, prefix, first, block
        )
        value_rows = lax.dynamic_slice_in_dim(values, begin, SEQ_LEN, 0)
        grad_rows = lax.dynamic_slice_in_dim(grad_mixed, first, block, 0)
        totals = lax.dynamic_slice_in_dim(log_total, first, block, 0)
        shares = jnp.exp(scores - jnp.transpose(totals)[:, :, None])
        grad_shares = jnp.einsum(
            "qhd,khd->hqk", grad_rows, value_rows, preferred_element_type=jnp.float32
        )
        inner = jnp.sum(shares * grad_shares, axis=-1, keepdims=True)
        grad_scores = (shares * (grad_shares - inner) * scale).astype(jnp.bfloat16)
        grad_query = jnp.einsum(
            "hqk,khd->qhd", grad_scores, key_rows, preferred_element_type=jnp.float32
        )
        grad_key = jnp.einsum(
            "hqk,qhd->khd", grad_scores, query_rows, preferred_element_type=jnp.float32
        )
        grad_value = jnp.einsum(
            "hqk,qhd->khd",
            shares.astype(jnp.bfloat16),
            grad_rows,
            preferred_element_type=jnp.float32,
        )
        grad_keys = lax.dynamic_update_slice_in_dim(
            grad_keys, lax.dynamic_slice_in_dim(grad_keys, begin, SEQ_LEN, 0) + grad_key, begin, 0
        )
        grad_values = lax.dynamic_update_slice_in_dim(
            grad_values,
            lax.dynamic_slice_in_dim(grad_values, begin, SEQ_LEN, 0) + grad_value,
            begin,
            0,
        )
        return ((grad_keys, grad_values), grad_query)

    empty = jnp.zeros((tokens, heads, width), jnp.float32)
    (grad_keys, grad_values), grad_queries = lax.scan(
        one_block, (empty, empty), jnp.arange(tokens // block, dtype=jnp.int32)
    )
    return (grad_queries.reshape(tokens, heads, width), grad_keys, grad_values)


def expert_slots(routes, valid_all, gates):
    numbers = jnp.arange(EXP_FFN, dtype=jnp.int32)
    hit = routes[:, None, :] == numbers[None, :, None]
    used = jnp.any(hit, axis=-1)
    weight = jnp.sum(jnp.where(hit, gates[:, None, :], 0.0), axis=-1) * valid_all[:, None]
    order = jnp.argsort(jnp.where(used, 0, 1).T.astype(jnp.int32), axis=1, stable=True)[:, :CAP]
    live = jnp.take_along_axis(used.T, order, axis=1)
    scale = jnp.where(live, jnp.take_along_axis(weight.T, order, axis=1), 0.0)
    return (order, scale)


def shards(
    stream,
    cotangent,
    gain_attention,
    w_inputs,
    w_output,
    gain_experts,
    w_router,
    w_carry,
    w_gate_up,
    w_down,
    w_constant,
    constant_vectors,
    previous_logits,
    routes,
    valid,
    prefix,
):
    shard_rows, width = stream.shape
    tokens = routes.shape[0]
    columns = w_inputs.shape[2]
    heads = columns // HEAD_DIM
    first_row = lax.axis_index("tensor") * shard_rows
    valid_all = valid.astype(jnp.float32)
    valid_here = lax.dynamic_slice_in_dim(valid_all, first_row, shard_rows, 0)
    routes_here = lax.dynamic_slice_in_dim(routes, first_row, shard_rows, 0)
    previous_here = lax.dynamic_slice_in_dim(previous_logits, first_row, shard_rows, 0)
    normed_here, inverse_one = norm_forward(stream, gain_attention)
    normed = lax.all_gather(normed_here.astype(jnp.bfloat16), "tensor", axis=0, tiled=True)
    linear = jnp.einsum(
        "td,sdc->stc", normed, w_inputs, preferred_element_type=jnp.float32
    ).reshape(3, tokens, heads, HEAD_DIM)
    cosine, sine = tables(tokens)
    queries = rotate(linear[0], cosine, sine).astype(jnp.bfloat16)
    keys = rotate(linear[1], cosine, sine).astype(jnp.bfloat16)
    values = linear[2].astype(jnp.bfloat16)
    mixed, log_total = attention_forward(queries, keys, values, valid, prefix)
    mixed = mixed.reshape(tokens, columns).astype(jnp.bfloat16)
    attention = lax.psum_scatter(
        jnp.dot(mixed, w_output, preferred_element_type=jnp.float32).astype(jnp.bfloat16),
        "tensor",
        scatter_dimension=0,
        tiled=True,
    ).astype(jnp.float32)
    middle = stream + attention
    second, inverse_two = norm_forward(middle, gain_experts)
    second_low = second.astype(jnp.bfloat16)
    second_rows = lax.all_gather(second_low, "tensor", axis=0, tiled=True)
    logits = jnp.dot(second_rows, w_router, preferred_element_type=jnp.float32) + jnp.dot(
        previous_logits, w_carry, precision=HIGHEST, preferred_element_type=jnp.float32
    )
    gates = jax.nn.softmax(jnp.take_along_axis(logits, routes, axis=1), axis=-1)
    order, scale = expert_slots(routes, valid_all, gates)
    flat = order.reshape(-1)
    inputs = second_rows[order]
    both = jnp.einsum("ecd,edgf->ecgf", inputs, w_gate_up, preferred_element_type=jnp.float32)
    sigma = jax.nn.sigmoid(both[:, :, 0])
    hidden = (both[:, :, 0] * sigma * both[:, :, 1]).astype(jnp.bfloat16)
    outputs = jnp.einsum("ecf,efd->ecd", hidden, w_down, preferred_element_type=jnp.float32)
    feed_part = (
        jnp.zeros((tokens, width), jnp.float32)
        .at[flat]
        .add((outputs * scale[:, :, None]).reshape(-1, width))
    )
    feed = lax.psum_scatter(
        feed_part.astype(jnp.bfloat16), "tensor", scatter_dimension=0, tiled=True
    ).astype(jnp.float32)
    gates_here = lax.dynamic_slice_in_dim(gates, first_row, shard_rows, 0)
    copy_gate = (
        jnp.sum(jnp.where(routes_here == EXP_FFN + 1, gates_here, 0.0), axis=-1) * valid_here
    )
    constant_gates = (
        jnp.stack(
            [
                jnp.sum(jnp.where(routes_here == EXP_FFN + 2 + index, gates_here, 0.0), axis=-1)
                for index in range(2)
            ],
            axis=1,
        )
        * valid_here[:, None]
    )
    alphas = jax.nn.softmax(
        jnp.einsum(
            "td,cad->tca", second, w_constant, precision=HIGHEST, preferred_element_type=jnp.float32
        ),
        axis=-1,
    )
    constant_out = (
        alphas[:, :, 0:1] * second[:, None, :] + alphas[:, :, 1:2] * constant_vectors[None, :, :]
    )
    experts = (
        feed
        + copy_gate[:, None] * second
        + jnp.sum(constant_gates[:, :, None] * constant_out, axis=1)
    )
    block_out = middle + experts
    squares = jnp.stack(
        [jnp.sum(valid_here[:, None] * part * part) for part in (block_out, attention, experts)]
    )
    counted = jnp.sum(valid_here)
    squares, counted = lax.psum((squares, counted), ("dp", "tensor"))
    upstream = lax.all_gather(cotangent.astype(jnp.bfloat16), "tensor", axis=0, tiled=True).astype(
        cotangent.dtype
    )
    upstream_rows = upstream[order]
    grad_rows = (upstream_rows * scale[:, :, None]).astype(jnp.bfloat16)
    gate_terms = jnp.sum(upstream_rows * outputs, axis=-1)
    numbers = jnp.arange(EXP_FFN, dtype=jnp.int32)
    gate_part = (
        jnp.zeros((tokens, EXP_FFN), jnp.float32).at[order, numbers[:, None]].add(gate_terms)
    )
    grad_hidden = jnp.einsum("ecd,efd->ecf", grad_rows, w_down, preferred_element_type=jnp.float32)
    grad_gate = grad_hidden * both[:, :, 1] * sigma * (1.0 + both[:, :, 0] * (1.0 - sigma))
    grad_up = grad_hidden * both[:, :, 0] * sigma
    grad_both = jnp.stack([grad_gate, grad_up], axis=2).astype(jnp.bfloat16)
    grad_down = jnp.einsum("ecf,ecd->efd", hidden, grad_rows, preferred_element_type=jnp.float32)
    grad_gate_up = jnp.einsum(
        "ecd,ecgf->edgf", inputs, grad_both, preferred_element_type=jnp.float32
    )
    grad_buffer = jnp.einsum(
        "ecgf,edgf->ecd", grad_both, w_gate_up, preferred_element_type=jnp.float32
    )
    second_part = (
        jnp.zeros((tokens, width), jnp.float32).at[flat].add(grad_buffer.reshape(-1, width))
    )
    grad_second, gate_grads = (
        lax.psum_scatter(
            second_part.astype(jnp.bfloat16), "tensor", scatter_dimension=0, tiled=True
        ).astype(jnp.float32),
        lax.psum_scatter(
            gate_part.astype(jnp.bfloat16), "tensor", scatter_dimension=0, tiled=True
        ).astype(jnp.float32),
    )
    copy_terms = jnp.sum(cotangent * second, axis=-1)
    constant_terms = jnp.sum(cotangent[:, None, :] * constant_out, axis=-1)
    table = jnp.concatenate(
        [gate_grads, jnp.zeros((shard_rows, 1), jnp.float32), copy_terms[:, None], constant_terms],
        axis=1,
    )
    picked = routes_here[:, :, None] == jnp.arange(EXP_FFN + 4, dtype=jnp.int32)[None, None, :]
    grad_gates = jnp.sum(jnp.where(picked, table[:, None, :], 0.0), axis=-1) * valid_here[:, None]
    grad_chosen = gates_here * (
        grad_gates - jnp.sum(gates_here * grad_gates, axis=-1, keepdims=True)
    )
    grad_logits = jnp.sum(jnp.where(picked, grad_chosen[:, :, None], 0.0), axis=1)
    grad_router = jnp.dot(
        second_low.astype(jnp.float32).T,
        grad_logits,
        precision=HIGHEST,
        preferred_element_type=jnp.float32,
    )
    grad_carry = jnp.dot(
        previous_here.T, grad_logits, precision=HIGHEST, preferred_element_type=jnp.float32
    )
    grad_previous = jnp.dot(
        grad_logits, w_carry.T, precision=HIGHEST, preferred_element_type=jnp.float32
    )
    grad_second = grad_second + jnp.dot(
        grad_logits,
        w_router.astype(jnp.float32).T,
        precision=HIGHEST,
        preferred_element_type=jnp.float32,
    )
    grad_second = grad_second + copy_gate[:, None] * cotangent
    grad_constant_out = constant_gates[:, :, None] * cotangent[:, None, :]
    grad_second = grad_second + jnp.sum(alphas[:, :, 0:1] * grad_constant_out, axis=1)
    grad_vectors = jnp.sum(alphas[:, :, 1:2] * grad_constant_out, axis=0)
    grad_alphas = jnp.stack(
        [
            jnp.sum(grad_constant_out * second[:, None, :], axis=-1),
            jnp.sum(grad_constant_out * constant_vectors[None, :, :], axis=-1),
        ],
        axis=-1,
    )
    grad_mix = alphas * (grad_alphas - jnp.sum(alphas * grad_alphas, axis=-1, keepdims=True))
    grad_second = grad_second + jnp.einsum(
        "tca,cad->td", grad_mix, w_constant, precision=HIGHEST, preferred_element_type=jnp.float32
    )
    grad_constant = jnp.einsum(
        "tca,td->cad", grad_mix, second, precision=HIGHEST, preferred_element_type=jnp.float32
    )
    grad_middle_norm, grad_gain_experts = norm_backward(
        middle, inverse_two, gain_experts, grad_second
    )
    grad_middle = cotangent + grad_middle_norm
    grad_attention = lax.all_gather(grad_middle.astype(jnp.bfloat16), "tensor", axis=0, tiled=True)
    grad_output = jnp.einsum("tc,td->cd", mixed, grad_attention, preferred_element_type=jnp.float32)
    grad_mixed = (
        jnp.dot(grad_attention, w_output.T, preferred_element_type=jnp.float32)
        .astype(jnp.bfloat16)
        .reshape(tokens, heads, HEAD_DIM)
    )
    grad_queries, grad_keys, grad_values = attention_backward(
        queries, keys, values, valid, prefix, log_total, grad_mixed
    )
    grad_linear = (
        jnp.stack(
            [rotate(grad_queries, cosine, -sine), rotate(grad_keys, cosine, -sine), grad_values]
        )
        .reshape(3, tokens, columns)
        .astype(jnp.bfloat16)
    )
    grad_inputs = jnp.einsum("td,stc->sdc", normed, grad_linear, preferred_element_type=jnp.float32)
    grad_normed = lax.psum_scatter(
        jnp.einsum("stc,sdc->td", grad_linear, w_inputs, preferred_element_type=jnp.float32).astype(
            jnp.bfloat16
        ),
        "tensor",
        scatter_dimension=0,
        tiled=True,
    ).astype(jnp.float32)
    grad_stream_norm, grad_gain_attention = norm_backward(
        stream, inverse_one, gain_attention, grad_normed
    )
    grad_stream = grad_middle + grad_stream_norm
    grad_inputs, grad_output, grad_gate_up, grad_down = (
        lax.psum(grad_inputs.astype(jnp.bfloat16), "dp").astype(jnp.float32),
        lax.psum(grad_output.astype(jnp.bfloat16), "dp").astype(jnp.float32),
        lax.psum(grad_gate_up.astype(jnp.bfloat16), "dp").astype(jnp.float32),
        lax.psum(grad_down.astype(jnp.bfloat16), "dp").astype(jnp.float32),
    )
    grad_gain_attention, grad_gain_experts, grad_router, grad_carry, grad_constant, grad_vectors = (
        lax.psum(
            (
                grad_gain_attention,
                grad_gain_experts,
                grad_router,
                grad_carry,
                grad_constant,
                grad_vectors,
            ),
            ("dp", "tensor"),
        )
    )
    rms_values = jnp.sqrt(squares / (jnp.maximum(counted, 1.0) * width))
    return (
        block_out,
        grad_stream,
        grad_gain_attention,
        grad_inputs,
        grad_output,
        grad_gain_experts,
        grad_router,
        grad_carry,
        grad_gate_up,
        grad_down,
        grad_constant,
        grad_vectors,
        grad_previous,
        rms_values,
    )


def solution(mesh):
    return jax.shard_map(
        shards,
        mesh=mesh,
        in_specs=(
            P(("dp", "tensor"), None),
            P(("dp", "tensor"), None),
            P(),
            P(None, None, "tensor"),
            P("tensor", None),
            P(),
            P(),
            P(),
            P(None, None, None, "tensor"),
            P(None, "tensor", None),
            P(),
            P(),
            P("dp", None),
            P("dp", None),
            P("dp"),
            P("dp"),
        ),
        out_specs=(
            P(("dp", "tensor"), None),
            P(("dp", "tensor"), None),
            P(),
            P(None, None, "tensor"),
            P("tensor", None),
            P(),
            P(),
            P(),
            P(None, None, None, "tensor"),
            P(None, "tensor", None),
            P(),
            P(),
            P(("dp", "tensor"), None),
            P(),
        ),
        check_vma=False,
    )
```

profile of v0, /device:TPU:0, one launch (start us, length us, event | category | flops | bytes accessed | tf_op | source)
XLA Modules:
  0.0 1210.8 jit_solution(15796279209822083464)
XLA Ops:
  15.3 64.5 %all-gather.5.cloned.1.call-done = bf16[2048,768]{1,0:T(8,128)(2,1)} async-done(((bf16[512,768]{1,0:T(8,128)(2,1)}), bf16[2048,768]{1,0:T(8,128)(2,1)}) %all-gather.5.cloned.1.call-update) | async-done | bytes 3145744 | tf_op jit(solution)/shard_map/all_gather | solution.py:178
  79.8 3.9 fusion.171
  86.8 44.7 %while.30 = (s32[]{:T(128)}, bf16[4,512,3,64]{1,3,2,0:T(8,128)(2,1)S(1)}, f32[4,512,3]{1,2,0:T(4,128)}, s32[4]{0:T(128)S(1)}, bf16[2048,3,64]{0,2,1:T(8,128)(2,1...) while((s32[]{:T(128)}, ...), condition=%wide.region_4.5_spmd, body=%wide.region_1.4_spmd.sunk | while | flops 424150048 | bytes 22415868 | solution.py:85
  105.5 3.1 fusion.229
  116.6 3.1 fusion.229
  141.2 53.8 %reduce-scatter.6.cloned.1.call-done = bf16[512,768]{1,0:T(8,128)(2,1)} async-done(((bf16[2048,768]{1,0:T(8,128)(2,1)}), bf16[512,768]{1,0:T(8,128)(2,1)}) %reduce-scatter.6.cloned.1.call-update) | async-done | bytes 786448 | tf_op jit(solution)/shard_map/reduce_scatter | solution.py:188
  204.1 38.2 %gather_fusion.2 = pred[4608]{0:T(1024)(128)(4,1)S(1)} fusion(pred[6,2048]{0,1:T(8,128)(4,1)S(1)} %bitcast.196, s32[4608]{0:T(1024)S(1)} %reshape.515), kind=kCustom, calls=%fused_computation.2 | custom fusion | bytes 46080 | tf_op jit(solution)/shard_map/jit(take_along_axis)/gather | solution.py:145
  244.5 19.0 %all-gather.7.cloned.1.call-done = bf16[2048,768]{1,0:T(8,128)(2,1)} async-done(((bf16[512,768]{1,0:T(8,128)(2,1)}), bf16[2048,768]{1,0:T(8,128)(2,1)}) %all-gather.7.cloned.1.call-update) | async-done | bytes 3145744 | tf_op jit(solution)/shard_map/all_gather | solution.py:197
  266.7 33.0 %gather_fusion.3 = f32[4096]{0:T(1024)S(1)} fusion(f32[2048,10]{0,1:T(8,128)S(1)} %convolution_add_fusion, s32[4096]{0:T(1024)S(1)} %reshape.521), kind=kCustom, calls=%fused_computation.3 | custom fusion | bytes 65536 | tf_op jit(solution)/shard_map/jit(take_along_axis)/gather | solution.py:201
  302.0 28.6 %gather_fusion.4 = f32[4608]{0:T(1024)S(1)} fusion(f32[6,2048]{1,0:T(8,128)S(1)} %multiply_bitcast_fusion, s32[4608]{0:T(1024)S(1)} %copy-done.2), kind=kCustom, calls=%fused_computation.4 | custom fusion | bytes 73728 | tf_op jit(solution)/shard_map/jit(take_along_axis)/gather | solution.py:146
  331.4 5.1 convert_element_type.168
  336.5 20.3 %gather_fusion.1 = f32[4608,768]{1,0:T(8,128)} fusion(f32[2048,768]{1,0:T(8,128)} %convert_element_type.168, s32[5120]{0:T(1024)S(1)} %copy-done.28), kind=kCustom, calls=%fused_computation.1 | custom fusion | bytes 28329984 | tf_op jit(solution)/shard_map/gather | solution.py:254
  356.8 19.8 %gather_fusion = bf16[4608,768]{1,0:T(8,128)(2,1)} fusion(bf16[2048,768]{1,0:T(8,128)(2,1)} %all-gather.7.cloned.1.call-done, s32[5120]{0:T(1024)S(1)} %copy-done.28), kind=kCustom, calls=%fused_computation | custom fusion | bytes 14174208 | tf_op jit(solution)/shard_map/gather | solution.py:204
  376.6 16.2 %fusion.101 = f32[6,768,2,512]{3,1,2,0:T(8,128)} fusion(bf16[6,768,768,1]{2,1,3,0:T(8,128)(2,1)} %bitcast.203, bf16[6,768,2,512]{3,2,1,0:T(2,128)(2,1)} %param.28), kind=kOutput, calls=%fused_computation.99 | convolution fusion | flops 7247757312 | bytes 35389440 | tf_op jit(solution)/shard_map/ecd,edgf->ecgf/dot_general | solution.py:205
  392.8 20.5 %fusion.107 = (bf16[6,768,1,512]{3,1,0,2:T(8,128)(2,1)}, bf16[6,768,1,512]{3,1,0,2:T(8,128)(2,1)}, bf16[6,768,512]{2,1,0:T(8,128)(2,1)}) fusion(f32[6,768,2,512]{3,1,2,0:T(8,128)} %fusion.101, bf16[6,512,768]{2,1,0:T(8,128)(2,1)} %param.29, f32[6,768,768]{2,1,0:T(8,128)} %bitcast.197, f32[6,768]{1,0:T(8,128)S(1)} %select_select_fusion), kind=kOutput, calls=%fused_computation.113 | convolution fusion | flops 3668705280 | bytes 51922944 | tf_op jit(solution)/shard_map/ecd,efd->ecf/dot_general | solution.py:261
  413.3 13.2 %broadcast_multiply_fusion = (f32[6,768,768]{2,1,0:T(8,128)}, f32[6,768]{1,0:T(8,128)S(1)}) fusion(f32[6,768]{1,0:T(8,128)S(1)} %select_select_fusion, f32[6,768,768]{2,1,0:T(8,128)} %bitcast.198, bf16[6,768,512]{2,1,0:T(8,128)(2,1)} %get-tuple-element.474, bf16[6,512,768]{2,1,0:T(8,128)(2,1)} %param.29), kind=kOutput, calls=%fused_computation.109 | convolution fusion | flops 3634490880 | bytes 37785600 | tf_op jit(solution)/shard_map/ecf,efd->ecd/dot_general | solution.py:208
  426.5 32.4 %scatter_custom_fusion.2 = f32[12288]{0:T(1024)S(1)} fusion(s32[4608]{0:T(1024)} %reshape.549, f32[4608]{0:T(1024)S(1)} %reshape.551, f32[]{:T(128)} %constant.252.clone.1), kind=kCustom, calls=%fused_computation.204 | custom fusion | flops 4608 | bytes 49664
  459.8 33.8 %scatter_custom_fusion = f32[2048,768]{1,0:T(8,128)} fusion(s32[4608]{0:T(1024)S(1)} %fusion.148, f32[4608,768]{1,0:T(8,128)} %bitcast.200, f32[]{:T(128)} %constant.252.clone.1), kind=kCustom, calls=%fused_computation.126 | custom fusion | flops 3538944 | bytes 6291968 | tf_op jit(solution)/shard_map/scatter-add | solution.py:212
  493.6 4.7 convert_element_type.165
  498.4 16.5 %fusion.99 = f32[6,768,768,1]{2,1,0,3:T(8,128)} fusion(bf16[6,768,2,512]{3,2,1,0:T(2,128)(2,1)} %param.28, bf16[6,768,1,512]{3,1,0,2:T(8,128)(2,1)} %get-tuple-element.473, bf16[6,768,1,512]{3,1,0,2:T(8,128)(2,1)} %get-tuple-element.472), kind=kOutput, calls=%fused_computation.97 | convolution fusion | flops 7252475904 | bytes 33030144 | tf_op jit(solution)/shard_map/ecgf,edgf->ecd/dot_general | solution.py:269
  514.9 33.8 %scatter_custom_fusion.1 = f32[2048,768]{1,0:T(8,128)} fusion(s32[4608]{0:T(1024)S(1)} %fusion.148, f32[4608,768]{1,0:T(8,128)} %bitcast.225, f32[]{:T(128)} %constant.252.clone.1), kind=kCustom, calls=%fused_computation.124 | custom fusion | flops 3538944 | bytes 6291968 | tf_op jit(solution)/shard_map/scatter-add | solution.py:273
  548.8 4.8 convert_element_type.170
  557.7 6.1 multiply_reduce_fusion.2
  567.4 53.2 %reduce-scatter.10.cloned.1.call-done = bf16[512,768]{1,0:T(8,128)(2,1)} async-done(((bf16[2048,768]{1,0:T(8,128)(2,1)}), bf16[512,768]{1,0:T(8,128)(2,1)}) %reduce-scatter.10.cloned.1.call-update) | async-done | bytes 786448 | tf_op jit(solution)/shard_map/reduce_scatter | solution.py:276
  620.6 6.8 multiply_reduce_fusion.4
  629.4 63.6 %all-gather.11.cloned.1.call-done = bf16[2048,768]{1,0:T(8,128)(2,1)} async-done(((bf16[512,768]{1,0:T(8,128)(2,1)}), bf16[2048,768]{1,0:T(8,128)(2,1)}) %all-gather.11.cloned.1.call-update) | async-done | bytes 3145744 | tf_op jit(solution)/shard_map/all_gather | solution.py:335
  693.0 3.9 convolution_convert_fusion.2
  699.7 222.5 %while.31 = (s32[]{:T(128)}, f32[2048,3,64]{0,2,1:T(8,128)}, f32[2048,3,64]{0,2,1:T(8,128)}, f32[4,512,3,64]{1,0,3,2:T(4,128)}, s32[4]{0:T(128)S(1)}, /*index=5*...) while((s32[]{:T(128)}, f32[2048,3,64]{0,2,1:T(8,128)}, ...), condition=%wide.region_37.38_spmd, body=%wide.region_35.37_spmd.sunk | while | flops 1050549760 | bytes 79493680 | solution.py:133
  700.9 4.8 fusion.240
  705.8 4.8 fusion.241
  713.2 14.6 %fusion.243 = f32[2048,3,64]{0,2,1:T(8,128)} fusion(f32[2048,3,64]{0,2,1:T(8,128)} %get-tuple-element.728, s32[]{:T(128)S(6)} %select_n.335, f32[3,512,1024]{2,1,0:T(8,128)} %fusion.240, f32[3,512,1024]{2,1,0:T(8,128)} %fusion.241, f32[3,512]{1,0:T(4,128)S(1)} %dynamic-slice_bitcast_fusion.2, pred[512,1024]{1,0:T(8,128)(4,1)S(1)} %fusion.242, ...), kind=kOutput, calls=%fused_computation.59.clone.1 | convolution fusion | flops 218827264 | bytes 28000264 | tf_op jit(solution)/shard_map/while/body/eval_jaxpr/hqk,qhd->khd/dot_general | solution.py:112
  727.8 5.7 fusion.244
  733.5 12.8 %fusion.245 = f32[1,512,3,64]{1,3,2,0:T(8,128)S(1)} fusion(f32[3,512,1024]{2,1,0:T(8,128)} %fusion.240, f32[3,512,1024]{2,1,0:T(8,128)} %fusion.241, f32[3,512]{1,0:T(4,128)S(1)} %dynamic-slice_bitcast_fusion.2, pred[512,1024]{1,0:T(8,128)(4,1)S(1)} %fusion.242, bf16[2048,3,64]{0,2,1:T(8,128)(2,1)} %get-tuple-element.756, s32[]{:T(128)S(6)} %select_n.335), kind=kOutput, calls=%fused_computation.62.clone.1 | convolution fusion | flops 218630656 | bytes 27017220 | tf_op jit(solution)/shard_map/while/body/eval_jaxpr/hqk,khd->qhd/dot_general | solution.py:109
  746.7 8.6 dynamic_update_slice.45
  756.6 4.8 fusion.240
  761.4 4.8 fusion.241
  768.9 14.5 %fusion.243 = f32[2048,3,64]{0,2,1:T(8,128)} fusion(f32[2048,3,64]{0,2,1:T(8,128)} %get-tuple-element.728, s32[]{:T(128)S(6)} %select_n.335, f32[3,512,1024]{2,1,0:T(8,128)} %fusion.240, f32[3,512,1024]{2,1,0:T(8,128)} %fusion.241, f32[3,512]{1,0:T(4,128)S(1)} %dynamic-slice_bitcast_fusion.2, pred[512,1024]{1,0:T(8,128)(4,1)S(1)} %fusion.242, ...), kind=kOutput, calls=%fused_computation.59.clone.1 | convolution fusion | flops 218827264 | bytes 28000264 | tf_op jit(solution)/shard_map/while/body/eval_jaxpr/hqk,qhd->khd/dot_general | solution.py:112
  783.4 5.7 fusion.244
  789.1 12.8 %fusion.245 = f32[1,512,3,64]{1,3,2,0:T(8,128)S(1)} fusion(f32[3,512,1024]{2,1,0:T(8,128)} %fusion.240, f32[3,512,1024]{2,1,0:T(8,128)} %fusion.241, f32[3,512]{1,0:T(4,128)S(1)} %dynamic-slice_bitcast_fusion.2, pred[512,1024]{1,0:T(8,128)(4,1)S(1)} %fusion.242, bf16[2048,3,64]{0,2,1:T(8,128)(2,1)} %get-tuple-element.756, s32[]{:T(128)S(6)} %select_n.335), kind=kOutput, calls=%fused_computation.62.clone.1 | convolution fusion | flops 218630656 | bytes 27017220 | tf_op jit(solution)/shard_map/while/body/eval_jaxpr/hqk,khd->qhd/dot_general | solution.py:109
  802.3 8.6 dynamic_update_slice.45
  812.2 4.8 fusion.240
  817.0 4.8 fusion.241
  824.5 14.5 %fusion.243 = f32[2048,3,64]{0,2,1:T(8,128)} fusion(f32[2048,3,64]{0,2,1:T(8,128)} %get-tuple-element.728, s32[]{:T(128)S(6)} %select_n.335, f32[3,512,1024]{2,1,0:T(8,128)} %fusion.240, f32[3,512,1024]{2,1,0:T(8,128)} %fusion.241, f32[3,512]{1,0:T(4,128)S(1)} %dynamic-slice_bitcast_fusion.2, pred[512,1024]{1,0:T(8,128)(4,1)S(1)} %fusion.242, ...), kind=kOutput, calls=%fused_computation.59.clone.1 | convolution fusion | flops 218827264 | bytes 28000264 | tf_op jit(solution)/shard_map/while/body/eval_jaxpr/hqk,qhd->khd/dot_general | solution.py:112
  839.0 5.7 fusion.244
  844.7 12.8 %fusion.245 = f32[1,512,3,64]{1,3,2,0:T(8,128)S(1)} fusion(f32[3,512,1024]{2,1,0:T(8,128)} %fusion.240, f32[3,512,1024]{2,1,0:T(8,128)} %fusion.241, f32[3,512]{1,0:T(4,128)S(1)} %dynamic-slice_bitcast_fusion.2, pred[512,1024]{1,0:T(8,128)(4,1)S(1)} %fusion.242, bf16[2048,3,64]{0,2,1:T(8,128)(2,1)} %get-tuple-element.756, s32[]{:T(128)S(6)} %select_n.335), kind=kOutput, calls=%fused_computation.62.clone.1 | convolution fusion | flops 218630656 | bytes 27017220 | tf_op jit(solution)/shard_map/while/body/eval_jaxpr/hqk,khd->qhd/dot_general | solution.py:109
  857.9 8.6 dynamic_update_slice.45
  867.8 4.8 fusion.240
  872.6 4.8 fusion.241
  880.1 14.5 %fusion.243 = f32[2048,3,64]{0,2,1:T(8,128)} fusion(f32[2048,3,64]{0,2,1:T(8,128)} %get-tuple-element.728, s32[]{:T(128)S(6)} %select_n.335, f32[3,512,1024]{2,1,0:T(8,128)} %fusion.240, f32[3,512,1024]{2,1,0:T(8,128)} %fusion.241, f32[3,512]{1,0:T(4,128)S(1)} %dynamic-slice_bitcast_fusion.2, pred[512,1024]{1,0:T(8,128)(4,1)S(1)} %fusion.242, ...), kind=kOutput, calls=%fused_computation.59.clone.1 | convolution fusion | flops 218827264 | bytes 28000264 | tf_op jit(solution)/shard_map/while/body/eval_jaxpr/hqk,qhd->khd/dot_general | solution.py:112
  894.6 5.7 fusion.244
  900.3 12.8 %fusion.245 = f32[1,512,3,64]{1,3,2,0:T(8,128)S(1)} fusion(f32[3,512,1024]{2,1,0:T(8,128)} %fusion.240, f32[3,512,1024]{2,1,0:T(8,128)} %fusion.241, f32[3,512]{1,0:T(4,128)S(1)} %dynamic-slice_bitcast_fusion.2, pred[512,1024]{1,0:T(8,128)(4,1)S(1)} %fusion.242, bf16[2048,3,64]{0,2,1:T(8,128)(2,1)} %get-tuple-element.756, s32[]{:T(128)S(6)} %select_n.335), kind=kOutput, calls=%fused_computation.62.clone.1 | convolution fusion | flops 218630656 | bytes 27017220 | tf_op jit(solution)/shard_map/while/body/eval_jaxpr/hqk,khd->qhd/dot_general | solution.py:109
  913.6 8.6 dynamic_update_slice.45
  924.6 3.1 reshape.493
  931.3 4.2 bitcast_convert_fusion
  935.6 13.4 %convolution_convert_fusion.1 = bf16[6,512,768]{2,1,0:T(8,128)(2,1)} fusion(bf16[6,768,512]{2,1,0:T(8,128)(2,1)} %get-tuple-element.474, f32[6,768,768]{2,1,0:T(8,128)} %bitcast.199, f32[6,768]{1,0:T(8,128)S(1)} %select_select_fusion), kind=kOutput, calls=%fused_computation.128 | convolution fusion | flops 3633315840 | bytes 23611392 | tf_op jit(solution)/shard_map/ecf,ecd->efd/dot_general | solution.py:265
  949.0 14.5 %fusion.103 = bf16[6,768,2,512]{3,1,2,0:T(8,128)(2,1)} fusion(bf16[6,768,768,1]{2,1,3,0:T(8,128)(2,1)} %bitcast.204, bf16[6,768,1,512]{3,1,0,2:T(8,128)(2,1)} %get-tuple-element.473, bf16[6,768,1,512]{3,1,0,2:T(8,128)(2,1)} %get-tuple-element.472), kind=kOutput, calls=%fused_computation.110 | convolution fusion | flops 7257194496 | bytes 25952256 | tf_op jit(solution)/shard_map/ecd,ecgf->edgf/dot_general | solution.py:266
  963.5 3.5 convolution_convert_fusion.3
  967.1 4.8 fusion.136
  977.3 17.3 %reduce-scatter.14.cloned.1.call-done = bf16[512,768]{1,0:T(8,128)(2,1)} async-done(((bf16[2048,768]{1,0:T(8,128)(2,1)}), bf16[512,768]{1,0:T(8,128)(2,1)}) %reduce-scatter.14.cloned.1.call-update) | async-done | bytes 786448 | tf_op jit(solution)/shard_map/reduce_scatter | solution.py:353
  997.0 43.2 %all-reduce = (f32[768]{0:T(1024)}, f32[768]{0:T(1024)}, f32[768,10]{0,1:T(8,128)}, f32[10,10]{1,0:T(8,128)}, f32[2,2,768]{2,1,0:T(2,128)}, /*index=5*/f32[2,768]{1,0:T(2,128)}, f32[3]{0:T(128)S(1)}, f32[]{:T(128)}) all-reduce(f32[768]{0:T(1024)S(1)} %get-tuple-element.390, ...), channel_id=1, replica_groups=mesh['dp'=8,'tensor'=4] {'dp','tensor'}, use_global_device_ids=true, to_apply=%region_41.42 | all-reduce | flops 13928 | bytes 111424 | tf_op jit(solution)/shard_map/psum | solution.py:372
  1041.4 3.3 fusion.122
  1044.7 130.0 %all-reduce.4.cloned.1.call-done = (bf16[6,768,2,512]{3,1,2,0:T(8,128)(2,1)}, bf16[3,768,192]{1,2,0:T(8,128)(2,1)}, bf16[192,768]{1,0:T(8,128)(2,1)}, bf16[6,512,768]{2,1,0:T(8,128)(2,1)}) async-done(((bf16[6,768,2,512]{3,1,2,0:T(8,128)(2,1)}, bf16[3,768,192]{1,2,0:T(8,128)(2,1)}, bf16[192,768]{1,0:T(8,128)(2,1)}, bf16[6,512,768]{2,1,0:T(8,128)(2,1)}), (bf16[6,768,2,512]{3,1,2,0:T(8,128)(2,1)}, ...) | async-done | bytes 15335440 | tf_op jit(solution)/shard_map/psum | solution.py:368
  1179.2 19.7 %copy.158 = f32[6,768,2,512]{3,2,1,0:T(2,128)} copy(bf16[6,768,2,512]{3,1,2,0:T(8,128)(2,1)} %get-tuple-element.452) | data formatting | bytes 28311552
  1198.9 4.6 convert_element_type.186
  (299 shorter events, 119.0 us)
Async XLA Ops:
  8.0 71.7 %copy-start = (bf16[3,768,192]{1,2,0:T(8,128)(2,1)S(1)}, bf16[3,768,192]{1,2,0:T(8,128)(2,1)}, u32[]{:S(2)}) copy-start(bf16[3,768,192]{1,2,0:T(8,128)(2,1)} %param.23) | copy-start | bytes 2654212
  8.0 71.7 %all-gather.5.cloned.1.call-start = ((), (), s32[]{:S(2)}) async-start(), calls=%async_computation.5 | async-start | bytes 3932160 | tf_op jit(solution)/shard_map/all_gather | solution.py:178
  13.4 181.6 %reduce-scatter.6.cloned.1.call-start = ((), (), s32[]{:S(2)}) async-start(), calls=%async_computation.6 | async-start | bytes 3932160 | tf_op jit(solution)/shard_map/reduce_scatter | solution.py:188
  15.3 69.8 %copy-start.13 = (f32[2048,32]{0,1:T(8,128)}, f32[2048,32]{0,1:T(8,128)S(1)}, u32[]{:S(2)}) copy-start(f32[2048,32]{0,1:T(8,128)S(1)} %get-tuple-element.500) | copy-start | bytes 786436
  85.0 1.8 copy-start.24
  85.0 1.8 copy-start.53
  131.5 1.7 copy-start.26
  135.9 59.1 %copy-start.5 = (f32[512,768]{1,0:T(8,128)S(1)}, f32[512,768]{1,0:T(8,128)}, u32[]{:S(2)}) copy-start(f32[512,768]{1,0:T(8,128)} %param.20) | copy-start | bytes 4718596
  135.9 66.0 %sort.19.cloned.1.call-start = ((), (), s32[]{:S(2)}) async-start(), calls=%async_computation.15 | async-start | bytes 393248 | tf_op jit(solution)/shard_map/jit(argsort)/sort | solution.py:144
  137.2 59.9 %copy-start.32 = (f32[768]{0:T(1024)S(1)}, f32[768]{0:T(1024)}, u32[]{:S(2)}) copy-start(f32[768]{0:T(1024)} %param.25) | copy-start | bytes 9220
  141.1 122.3 %all-gather.7.cloned.1.call-start = ((), (), s32[]{:S(2)}) async-start(), calls=%async_computation.7 | async-start | bytes 3932160 | tf_op jit(solution)/shard_map/all_gather | solution.py:197
  195.0 2.2 copy-start.7
  196.5 3.3 copy-start.3
  197.2 2.6 copy-start.36
  199.8 131.6 %all-gather.9.cloned.1.call-start = ((), (), s32[]{:S(2)}) async-start(), calls=%async_computation.9 | async-start | bytes 3932160 | tf_op jit(solution)/shard_map/all_gather | solution.py:251
  200.4 366.1 %reduce-scatter.12.cloned.1.call-start = ((), (), s32[]{:S(2)}) async-start(), calls=%async_computation.11 | async-start | bytes 40960 | tf_op jit(solution)/shard_map/reduce_scatter | solution.py:279
  204.1 38.3 %copy-start.1 = (s32[4608]{0:T(1024)}, s32[4608]{0:T(1024)S(1)}, u32[]{:S(2)}) copy-start(s32[4608]{0:T(1024)S(1)} %reshape.515) | copy-start | bytes 55300
  204.1 39.0 %copy-start.52 = (s32[2]{0:T(128)S(1)}, s32[2]{0:T(128)}, u32[]{:S(2)}) copy-start(s32[2]{0:T(128)} %constant.275) | copy-start | bytes 28
  204.1 39.0 %copy-start.51 = (s32[2]{0:T(128)S(1)}, s32[2]{0:T(128)}, u32[]{:S(2)}) copy-start(s32[2]{0:T(128)} %constant.278) | copy-start | bytes 28
  204.1 59.4 %copy-start.34 = (bf16[768,10]{0,1:T(8,128)(2,1)S(1)}, bf16[768,10]{0,1:T(8,128)(2,1)}, u32[]{:S(2)}) copy-start(bf16[768,10]{0,1:T(8,128)(2,1)} %param.26) | copy-start | bytes 46084
  242.4 23.9 %copy-start.29 = (f32[2048,10]{0,1:T(8,128)S(1)}, f32[2048,10]{0,1:T(8,128)}, u32[]{:S(2)}) copy-start(f32[2048,10]{0,1:T(8,128)} %param.32) | copy-start | bytes 245764
  242.4 23.9 %copy-start.44 = (f32[10,10]{1,0:T(8,128)S(1)}, f32[10,10]{1,0:T(8,128)}, u32[]{:S(2)}) copy-start(f32[10,10]{1,0:T(8,128)} %param.27) | copy-start | bytes 1204
  266.6 34.4 %copy-start.23 = (s32[2048,2]{0,1:T(2,128)S(1)}, s32[2048,2]{0,1:T(2,128)}, u32[]{:S(2)}) copy-start(s32[2048,2]{0,1:T(2,128)} %param.33) | copy-start | bytes 49156
  266.7 35.3 %copy-start.40 = (f32[2048]{0:T(1024)S(1)}, f32[2048]{0:T(1024)}, u32[]{:S(2)}) copy-start(f32[2048]{0:T(1024)} %convert_element_type.164) | copy-start | bytes 24580
  299.7 2.3 copy-start.2
  302.0 28.6 %copy-start.46 = (pred[6,768]{1,0:T(8,128)(4,1)S(1)}, pred[6,768]{1,0:T(8,128)(4,1)}, u32[]{:S(2)}) copy-start(pred[6,768]{1,0:T(8,128)(4,1)} %reshape.518) | copy-start | bytes 13828
  331.4 5.1 copy-start.28
  413.3 46.5 %copy-start.38 = (s32[1,1,6,768]{3,1,2,0:T(1,128)S(1)}, s32[1,1,6,768]{3,1,2,0:T(1,128)}, u32[]{:S(2)}) copy-start(s32[1,1,6,768]{3,1,2,0:T(1,128)} %copy.199) | copy-start | bytes 55300
  459.7 107.7 %reduce-scatter.8.cloned.1.call-start = ((), (), s32[]{:S(2)}) async-start(), calls=%async_computation.8 | async-start | bytes 3932160 | tf_op jit(solution)/shard_map/reduce_scatter | solution.py:214
  498.4 122.3 %reduce-scatter.10.cloned.1.call-start = ((), (), s32[]{:S(2)}) async-start(), calls=%async_computation.10 | async-start | bytes 3932160 | tf_op jit(solution)/shard_map/reduce_scatter | solution.py:276
  553.5 1.6 copy-start.4
  553.5 1.6 copy-start.33
  553.5 1.6 copy-start.37
  553.5 1.6 copy-start.39
  553.5 3.4 copy-start.31
  553.5 4.1 copy-start.50
  553.6 139.5 %all-gather.11.cloned.1.call-start = ((), (), s32[]{:S(2)}) async-start(), calls=%async_computation.12 | async-start | bytes 3932160 | tf_op jit(solution)/shard_map/all_gather | solution.py:335
  557.7 9.5 copy-start.48
  557.7 62.9 %copy-start.12 = (bf16[512,768]{1,0:T(8,128)(2,1)S(1)}, bf16[512,768]{1,0:T(8,128)(2,1)}, u32[]{:S(2)}) copy-start(bf16[512,768]{1,0:T(8,128)(2,1)} %reduce-scatter.6.cloned.1.call-done) | copy-start | bytes 2359300
  557.7 62.9 %copy-start.35 = (bf16[768,10]{0,1:T(8,128)(2,1)S(1)}, bf16[768,10]{0,1:T(8,128)(2,1)}, u32[]{:S(2)}) copy-start(bf16[768,10]{0,1:T(8,128)(2,1)} %param.26) | copy-start | bytes 46084
  620.6 6.9 copy-start.8
  620.6 6.9 copy-start.49
  627.5 65.6 %copy-start.27 = (bf16[192,768]{1,0:T(8,128)(2,1)S(1)}, bf16[192,768]{1,0:T(8,128)(2,1)}, u32[]{:S(2)}) copy-start(bf16[192,768]{1,0:T(8,128)(2,1)} %param.24) | copy-start | bytes 884740
  629.4 365.3 %reduce-scatter.14.cloned.1.call-start = ((), (), s32[]{:S(2)}) async-start(), calls=%async_computation.13 | async-start | bytes 3932160 | tf_op jit(solution)/shard_map/reduce_scatter | solution.py:353
  697.0 2.7 copy-start.25
  697.0 2.7 copy-start.54
  922.2 5.6 copy-start.14
  922.2 5.6 copy-start.15
  927.8 3.5 copy-start.20
  930.2 5.3 copy-start.16
  930.3 1.0 copy-start.18
  935.6 239.1 %all-reduce.4.cloned.1.call-start = ((), (), s32[]{:S(2)}) async-start(), calls=%async_computation.14 | async-start | bytes 30670848 | tf_op jit(solution)/shard_map/psum | solution.py:368
  949.0 14.5 %copy-start.10 = (bf16[24,8,4,512]{3,1,2,0:T(8,128)(2,1)S(1)}, bf16[24,8,4,512]{3,1,2,0:T(8,128)(2,1)}, u32[]{:S(2)}) copy-start(bf16[24,8,4,512]{3,1,2,0:T(8,128)(2,1)} %copy-done.9) | copy-start | bytes 2359300
  963.5 3.6 copy-start.17
  963.5 3.6 copy-start.19
  963.5 3.6 copy-start.21
  971.9 2.2 copy-start.45
  971.9 3.0 copy-start.11
  971.9 22.7 %copy-start.41 = (f32[768]{0:T(1024)S(1)}, f32[768]{0:T(1024)}, u32[]{:S(2)}) copy-start(f32[768]{0:T(1024)} %param.22) | copy-start | bytes 9220
  971.9 22.7 %copy-start.43 = (f32[512]{0:T(512)S(1)}, f32[512]{0:T(512)}, u32[]{:S(2)}) copy-start(f32[512]{0:T(512)} %copy-done.42) | copy-start | bytes 6148
  971.9 69.5 %copy-start.47 = (f32[512]{0:T(512)S(1)}, f32[512]{0:T(512)}, u32[]{:S(2)}) copy-start(f32[512]{0:T(512)} %get-tuple-element.503) | copy-start | bytes 6148
  973.0 68.4 %copy-start.6 = (f32[512,768]{1,0:T(8,128)S(1)}, f32[512,768]{1,0:T(8,128)}, u32[]{:S(2)}) copy-start(f32[512,768]{1,0:T(8,128)} %param.20) | copy-start | bytes 4718596
  1177.2 21.7 %slice-start = ((s8[4718592]{0:T(1024)(128)(4,1)}), s8[4194304]{0:T(1024)(128)(4,1)S(1)}, s32[]{:S(2)}) async-start(s8[4718592]{0:T(1024)(128)(4,1)} %bitcast.207), calls=%async_computation.17 | async-start | bytes 8388608
  1179.2 19.7 %slice-start.1 = ((s8[4718592]{0:T(1024)(128)(4,1)}), s8[524288]{0:T(1024)(128)(4,1)S(1)}, s32[]{:S(2)}) async-start(s8[4718592]{0:T(1024)(128)(4,1)} %bitcast.207), calls=%async_computation.18 | async-start | bytes 1048576
  (4 other events, 2.8 us)
Sparse Core Ops, SparseCore 0:
  13.5 66.1 all-gather.4
  136.0 58.8 reduce-scatter.5
  199.9 63.5 all-gather.6
  265.5 62.1 all-gather.8
  459.8 17.5 reduce-scatter.11
  498.5 58.8 reduce-scatter.7
  560.3 60.2 reduce-scatter.9
  629.5 63.5 all-gather.10
  935.7 58.8 reduce-scatter.13
Sparse Core Ops, SparseCore 1:
  141.2 3.3 sort.21.cloned.1.call-done
  972.0 202.6 all-reduce.3
  (1 shorter events, 0.0 us)
where the time goes:
time: 1220 us; the launch traced here: 1210 us
  waiting for transfers between devices  402 us (33%)
  matrix products  328 us (27%)
  local copies, waits for them, and re-layouts  228 us (19%)
  other arithmetic  186 us (15%)
  blocking collectives  43.2 us (4%)
  between operations  16.9 us (1%)
    psum x1, waiting for transfers between devices, shards(): lax.psum(grad_gate_up.astype(jnp.bfloat16), 'dp').astype(jnp.float32)  130 us
    all_gather x1, waiting for transfers between devices, shards(): lax.all_gather(normed_here.astype(jnp.bfloat16), 'tensor', axis=0, tiled=...  64.5 us
    all_gather x1, waiting for transfers between devices, shards(): lax.all_gather(grad_middle.astype(jnp.bfloat16), 'tensor', axis=0, tiled=...  63.6 us
    dot_general x4, matrix products, one_block(): jnp.einsum('hqk,qhd->khd', grad_scores, query_rows, preferred_element_typ...  58.2 us
    reduce_scatter x1, waiting for transfers between devices, shards(): lax.psum_scatter(jnp.dot(mixed, w_output, preferred_element_type=jnp.floa...  53.8 us
    reduce_scatter x1, waiting for transfers between devices, shards(): lax.psum_scatter(second_part.astype(jnp.bfloat16), 'tensor', scatter_dime...  53.2 us
    dot_general x4, matrix products, one_block(): jnp.einsum('hqk,khd->qhd', grad_scores, key_rows, preferred_element_type=...  51.2 us
    psum x1, blocking collectives, shards(): lax.psum((grad_gain_attention, grad_gain_experts, grad_router, grad_carry...  43.2 us
  transfers between devices with their start and end apart: 10, of which 7 were waited for; matrix products, arithmetic and copies ran while one was open for 22% of the time, Pallas kernels for 0%

commit v1 on v0

v1 whole, which is shorter than its diff:
```python
import functools

import jax
import jax.numpy as jnp
from jax import lax
from jax.experimental import pallas as pl
from jax.experimental.pallas import tpu as pltpu
from jax.sharding import PartitionSpec as P

HEAD_DIM = 64
EXP_FFN = 6
SEQ_LEN = 1024
EPSILON = 1e-05
HIGHEST = lax.Precision.HIGHEST
F32 = jnp.float32
BF16 = jnp.bfloat16
I32 = jnp.int32

LANES = 128
TILE = 128
QUERY_BLOCK = 256

SIDE = ((0, 1), (1, 0), (2, 3), (3, 2))
CROSS = ((0, 2), (1, 3), (2, 0), (3, 1))
MIDDLE = ((1, 2), (2, 1))
OUTWARD = ((1, 0), (2, 3))
INWARD = ((0, 1), (3, 2))


def dot(left, right):
    return jnp.dot(left, right, preferred_element_type=F32)


def dot_nt(left, right):
    return lax.dot_general(left, right, (((1,), (1,)), ((), ())), preferred_element_type=F32)


def dot_tn(left, right):
    return lax.dot_general(left, right, (((0,), (0,)), ((), ())), preferred_element_type=F32)


def norm_forward(values, gain):
    inverse = lax.rsqrt(jnp.mean(values * values, axis=-1, keepdims=True) + EPSILON)
    return (values * inverse * gain, inverse)


def norm_backward(values, inverse, gain, grad):
    scaled = grad * gain
    inner = jnp.mean(scaled * values, axis=-1, keepdims=True)
    return inverse * scaled - values * inverse**3 * inner


def along_z(value, pairs):
    return lax.ppermute(value, "tensor", pairs)


def along_dp(value, bit, size):
    return lax.ppermute(value, "dp", [(i, i ^ (1 << bit)) for i in range(size)])


def gather_rows(own, outer):
    side = along_z(own, SIDE)
    middle = along_z(own, MIDDLE)
    far = along_z(middle, OUTWARD)
    across = along_z(side, MIDDLE)
    last = along_z(across, OUTWARD)
    return (own, side, jnp.where(outer, far, middle), jnp.where(outer, last, across))


def slot_chunks(here):
    table = jnp.array([[0, 1, 2, 3], [1, 0, 2, 3], [2, 3, 1, 0], [3, 2, 1, 0]], I32)
    return lax.dynamic_slice_in_dim(table, here, 1, 0)[0]


def scatter_rows(parts):
    last = parts[3] + along_z(parts[3], INWARD)
    third = parts[2] + along_z(parts[2], INWARD)
    second = parts[1] + along_z(last, MIDDLE)
    return (
        parts[0].astype(F32)
        + along_z(third, MIDDLE).astype(F32)
        + along_z(second, SIDE).astype(F32)
    )


def reduce_blocks(value, bits, index, size):
    for bit in bits:
        half = value.shape[0] // 2
        mine = (index >> bit) & 1
        sent = lax.dynamic_slice_in_dim(value, (1 - mine) * half, half, 0)
        kept = lax.dynamic_slice_in_dim(value, mine * half, half, 0)
        value = kept + along_dp(sent, bit, size)
    return value


def spread_blocks(value, bits, index, size):
    for bit in reversed(bits):
        mine = (index >> bit) & 1
        other = along_dp(value, bit, size)
        value = jnp.where(
            mine == 0,
            jnp.concatenate([value, other], axis=0),
            jnp.concatenate([other, value], axis=0),
        )
    return value


def sum_everywhere(value, bits, size):
    for bit in bits:
        value = value + along_dp(value, bit, size)
    value = value + along_z(value, SIDE)
    return value + along_z(value, CROSS)


def rope_tables(offset):
    lane = jnp.arange(LANES, dtype=I32)
    row = jnp.arange(SEQ_LEN, dtype=I32)
    position = jnp.where(row < SEQ_LEN // 2, row + offset, row - offset).astype(F32)
    half = HEAD_DIM // 2
    frequency = 10000.0 ** (-(lane % half).astype(F32) / half)
    angles = position[:, None] * frequency[None, :]
    sign = jnp.where(lane % HEAD_DIM < half, -1.0, 1.0)
    return (jnp.cos(angles), jnp.sin(angles) * sign[None, :])


def swap_halves(value):
    half = HEAD_DIM // 2
    lane = lax.broadcasted_iota(I32, value.shape, 1)
    return jnp.where(
        lane % HEAD_DIM < half,
        pltpu.roll(value, LANES - half, 1),
        pltpu.roll(value, half, 1),
    )


def fill_bias(scalars, valid_ref, bias):
    offset, prefix = scalars[0], scalars[1]
    keys = lax.broadcasted_iota(I32, (SEQ_LEN, 1), 0)
    keys = jnp.where(keys < SEQ_LEN // 2, keys + offset, keys - offset)
    queries = lax.broadcasted_iota(I32, (1, SEQ_LEN), 1)
    queries = jnp.where(queries < SEQ_LEN // 2, queries + offset, queries - offset)
    seen = jnp.where(valid_ref[...] > 0, keys, SEQ_LEN)
    shown = ((seen <= queries) | (seen < prefix)) | (keys == queries)
    bias[...] = jnp.where(shown, 0.0, -1e30)


def head_lanes(value, head):
    lane = lax.broadcasted_iota(I32, value.shape, 1)
    return jnp.where((lane >= head * HEAD_DIM) & (lane < (head + 1) * HEAD_DIM), value, 0)


def attention_kernel(
    scalars, own, other, weights, w_out, cosine, sine, valid,
    part_own, part_other, queries, keys, values, mixed, totals,
    bias, key_rows, value_columns, total,
):
    step = pl.program_id(0)
    half = SEQ_LEN // 2
    upper, lower = pl.ds(0, half), pl.ds(half, half)

    @pl.when(step == 0)
    def _():
        fill_bias(scalars, valid, bias)
        total[...] = jnp.zeros_like(total)

    for source, rows in ((own, upper), (other, lower)):
        x = source[...]
        for kind, target in ((0, queries), (1, keys), (2, values)):
            y = dot_nt(x, weights[kind])
            if kind < 2:
                y = y * cosine[rows, :] + swap_halves(y) * sine[rows, :]
            target[rows, :] = y.astype(BF16)
    key_rows[...] = keys[...]
    value_columns[...] = values[...].T

    @pl.loop(0, SEQ_LEN // QUERY_BLOCK)
    def _(index):
        columns = pl.ds(pl.multiple_of(index * QUERY_BLOCK, QUERY_BLOCK), QUERY_BLOCK)
        query = queries[columns, :] * 0.125
        outs = []
        for head in range(2):
            scores = dot_nt(key_rows[...], head_lanes(query, head)) + bias[:, columns]
            top = jnp.max(scores, axis=0, keepdims=True)
            raw = jnp.exp(scores - top)
            summed = jnp.sum(raw, axis=0, keepdims=True)
            shares = (raw * (1.0 / summed)).astype(BF16)
            outs.append(dot(value_columns[head * HEAD_DIM : (head + 1) * HEAD_DIM, :], shares))
            totals[0, head : head + 1, columns] = top + jnp.log(summed)
        mixed[columns, :] = jnp.concatenate(outs, axis=0).T.astype(BF16)

    total[...] += dot(mixed[...], w_out[...])

    @pl.when(step == pl.num_programs(0) - 1)
    def _():
        part_own[...] = total[upper, :].astype(BF16)
        part_other[...] = total[lower, :].astype(BF16)


def attention_specs(pairs, width):
    whole = lambda *shape: pl.BlockSpec(shape, lambda p, s: (0,) * len(shape))
    half = SEQ_LEN // 2
    rows = whole(half, width)
    weights = pl.BlockSpec((3, LANES, width), lambda p, s: (0, p, 0))
    w_out = pl.BlockSpec((LANES, width), lambda p, s: (p, 0))
    table = whole(SEQ_LEN, LANES)
    column = pl.BlockSpec((SEQ_LEN, LANES), lambda p, s: (0, p))
    totals = pl.BlockSpec((1, 8, SEQ_LEN), lambda p, s: (p, 0, 0))
    return (rows, weights, w_out, table, whole(SEQ_LEN, 1), column, totals)


def attention_forward(scalars, own, other, weights, w_out, cosine, sine, valid):
    width = own.shape[1]
    pairs = weights.shape[1] // LANES
    rows, spec_w, spec_o, table, spec_v, column, totals = attention_specs(pairs, width)
    half = SEQ_LEN // 2
    shape = jax.ShapeDtypeStruct
    flops = 2 * SEQ_LEN * pairs * LANES * (4 * width + 4 * SEQ_LEN)
    return pl.pallas_call(
        attention_kernel,
        grid_spec=pltpu.PrefetchScalarGridSpec(
            num_scalar_prefetch=1,
            grid=(pairs,),
            in_specs=[rows, rows, spec_w, spec_o, table, table, spec_v],
            out_specs=[rows, rows, column, column, column, column, totals],
            scratch_shapes=[
                pltpu.VMEM((SEQ_LEN, SEQ_LEN), F32),
                pltpu.VMEM((SEQ_LEN, LANES), BF16),
                pltpu.VMEM((LANES, SEQ_LEN), BF16),
                pltpu.VMEM((SEQ_LEN, width), F32),
            ],
        ),
        out_shape=[
            shape((half, width), BF16),
            shape((half, width), BF16),
            *[shape((SEQ_LEN, pairs * LANES), BF16)] * 4,
            shape((pairs, 8, SEQ_LEN), F32),
        ],
        compiler_params=pltpu.CompilerParams(vmem_limit_bytes=48 * 2**20),
        cost_estimate=pl.CostEstimate(
            flops=flops, bytes_accessed=12 * 2**20, transcendentals=2 * pairs * SEQ_LEN**2
        ),
        name="attention_forward",
    )(scalars, own, other, weights, w_out, cosine, sine, valid)


def attention_back_kernel(
    scalars, own, other, weights, w_out, cosine, sine, valid,
    grad_own, grad_other, queries, keys, values, mixed, totals,
    part_own, part_other, grad_w, grad_o, gain_row,
    bias, grad_rows, key_columns, total, grad_q, grad_k, grad_v,
):
    step = pl.program_id(0)
    half = SEQ_LEN // 2
    upper, lower = pl.ds(0, half), pl.ds(half, half)

    @pl.when(step == 0)
    def _():
        fill_bias(scalars, valid, bias)
        total[...] = jnp.zeros_like(total)

    grad_rows[upper, :] = dot_nt(grad_own[...], w_out[...]).astype(BF16)
    grad_rows[lower, :] = dot_nt(grad_other[...], w_out[...]).astype(BF16)
    columns_mixed = mixed[...].T
    grad_o[...] = (
        dot(columns_mixed[:, :half], grad_own[...]) + dot(columns_mixed[:, half:], grad_other[...])
    ).astype(BF16)
    key_columns[...] = keys[...].T
    grad_k[...] = jnp.zeros_like(grad_k)
    grad_v[...] = jnp.zeros_like(grad_v)

    @pl.loop(0, SEQ_LEN // QUERY_BLOCK)
    def _(index):
        columns = pl.ds(pl.multiple_of(index * QUERY_BLOCK, QUERY_BLOCK), QUERY_BLOCK)
        query = queries[columns, :] * 0.125
        grad = grad_rows[columns, :]
        outs = []
        for head in range(2):
            query_head = head_lanes(query, head)
            grad_head = head_lanes(grad, head)
            scores = dot_nt(keys[...], query_head) + bias[:, columns]
            shares = jnp.exp(scores - totals[0, head : head + 1, columns])
            grad_shares = dot_nt(values[...], grad_head)
            grad_v[...] += dot(shares.astype(BF16), grad_head)
            product = shares * grad_shares
            inner = jnp.sum(product, axis=0, keepdims=True)
            grad_scores = (product - shares * inner).astype(BF16)
            grad_k[...] += dot(grad_scores, query_head)
            outs.append(dot(key_columns[head * HEAD_DIM : (head + 1) * HEAD_DIM, :], grad_scores))
        grad_q[columns, :] = jnp.concatenate(outs, axis=0).T * 0.125

    for kind, source in ((0, grad_q), (1, grad_k), (2, grad_v)):
        y = source[...]
        if kind < 2:
            y = y * cosine[...] - swap_halves(y) * sine[...]
        y = y.astype(BF16)
        total[...] += dot(y, weights[kind])
        columns_y = y.T
        grad_w[kind] = (
            dot(columns_y[:, :half], own[...]) + dot(columns_y[:, half:], other[...])
        ).astype(BF16)

    @pl.when(step == pl.num_programs(0) - 1)
    def _():
        part_own[...] = total[upper, :].astype(BF16)
        part_other[...] = total[lower, :].astype(BF16)
        product = total[upper, :] * own[...].astype(F32) + total[lower, :] * other[...].astype(F32)
        gain_row[...] = jnp.sum(product.reshape(half // 8, 8, product.shape[1]), axis=0)


def attention_backward(
    scalars, own, other, weights, w_out, cosine, sine, valid, grad_own, grad_other, saved
):
    width = own.shape[1]
    pairs = weights.shape[1] // LANES
    rows, spec_w, spec_o, table, spec_v, column, totals = attention_specs(pairs, width)
    half = SEQ_LEN // 2
    shape = jax.ShapeDtypeStruct
    flops = 2 * SEQ_LEN * pairs * LANES * (8 * width + 10 * SEQ_LEN)
    return pl.pallas_call(
        attention_back_kernel,
        grid_spec=pltpu.PrefetchScalarGridSpec(
            num_scalar_prefetch=1,
            grid=(pairs,),
            in_specs=[
                rows, rows, spec_w, spec_o, table, table, spec_v,
                rows, rows, column, column, column, column, totals,
            ],
            out_specs=[
                rows,
                rows,
                spec_w,
                spec_o,
                pl.BlockSpec((8, width), lambda p, s: (0, 0)),
            ],
            scratch_shapes=[
                pltpu.VMEM((SEQ_LEN, SEQ_LEN), F32),
                pltpu.VMEM((SEQ_LEN, LANES), BF16),
                pltpu.VMEM((LANES, SEQ_LEN), BF16),
                pltpu.VMEM((SEQ_LEN, width), F32),
                *[pltpu.VMEM((SEQ_LEN, LANES), F32)] * 3,
            ],
        ),
        out_shape=[
            shape((half, width), BF16),
            shape((half, width), BF16),
            shape((3, pairs * LANES, width), BF16),
            shape((pairs * LANES, width), BF16),
            shape((8, width), F32),
        ],
        compiler_params=pltpu.CompilerParams(vmem_limit_bytes=48 * 2**20),
        cost_estimate=pl.CostEstimate(
            flops=flops, bytes_accessed=20 * 2**20, transcendentals=2 * pairs * SEQ_LEN**2
        ),
        name="attention_backward",
    )(
        scalars, own, other, weights, w_out, cosine, sine, valid, grad_own, grad_other, *saved
    )


def most_tiles(rows):
    return (2 * rows + EXP_FFN * (TILE - 1)) // TILE


def expert_plan(routes, valid, chunks):
    tokens = routes.shape[0]
    rows = tokens // chunks
    tiles = most_tiles(rows)
    numbers = jnp.arange(8, dtype=I32)[:, None]
    named = ((routes[:, 0][None, :] == numbers) | (routes[:, 1][None, :] == numbers)) & (
        valid[None, :] > 0
    )
    named = (named & (numbers < EXP_FFN)).reshape(8 * chunks, rows)
    before = (jnp.arange(rows)[:, None] < jnp.arange(rows)[None, :]).astype(BF16)
    place = dot(named.astype(BF16), before).astype(I32)
    place = jnp.where(named, place, -1).reshape(8, chunks, rows)
    count = jnp.sum(named.astype(I32), axis=1).reshape(8, chunks)[:EXP_FFN]
    number = (count + TILE - 1) // TILE
    number = jnp.where(jnp.arange(chunks)[None, :] == 0, jnp.maximum(number, 1), number)
    earlier = jnp.arange(EXP_FFN)[:, None] > jnp.arange(EXP_FFN)[None, :]
    first = jnp.sum(jnp.where(earlier[:, :, None], number[None], 0), axis=1)
    total = jnp.sum(number, axis=0)
    slot = jnp.arange(tiles, dtype=I32)
    expert = jnp.sum((first + number)[:, :, None] <= slot, axis=0)
    expert = jnp.minimum(expert, EXP_FFN - 1)
    pick = jnp.arange(EXP_FFN)[:, None, None] == expert[None]
    base = (slot - jnp.sum(jnp.where(pick, first[:, :, None], 0), axis=0)) * TILE
    meta = jnp.concatenate([expert, base, total[:, None]], axis=1).astype(I32)
    flat = number.reshape(-1)
    groups = flat.shape[0]
    earlier = jnp.arange(groups)[:, None] > jnp.arange(groups)[None, :]
    start = jnp.sum(jnp.where(earlier, flat[None, :], 0), axis=1)
    everything = jnp.sum(flat)
    step = jnp.minimum(jnp.arange(chunks * tiles, dtype=I32), everything - 1)
    group = jnp.sum((start + flat)[:, None] <= step[None, :], axis=0)
    pick = jnp.arange(groups)[:, None] == group[None, :]
    offset = jnp.arange(chunks)[None, :] * tiles + first
    block = jnp.sum(jnp.where(pick, (offset.reshape(-1) - start)[:, None], 0), axis=0) + step
    walk = jnp.concatenate([group // chunks, block, everything[None]]).astype(I32)
    return (place.transpose(1, 0, 2), meta.reshape(-1), walk)


def expert_kernel(tiles, span, meta, chunk, x, cot, place, carry, routes, w_router, w_up, w_down, *refs):
    part, feed, x_rows, hidden_rows, grad_rows, both_rows, table, total = refs[-8:]
    step = pl.program_id(0)
    width = x.shape[1]
    hidden_width = w_down.shape[1]
    offset = chunk[0] * span

    @pl.when(step == 0)
    def _():
        logits = dot(x[...], w_router[...]) + carry[0]
        lane = lax.broadcasted_iota(I32, logits.shape, 1)
        one, two = lane == routes[0, :, 0:1], lane == routes[0, :, 1:2]
        score_one = jnp.sum(jnp.where(one, logits, 0.0), axis=1, keepdims=True)
        score_two = jnp.sum(jnp.where(two, logits, 0.0), axis=1, keepdims=True)
        top = jnp.maximum(score_one, score_two)
        score_one, score_two = jnp.exp(score_one - top), jnp.exp(score_two - top)
        both = score_one + score_two
        gates = jnp.where(one, score_one / both, 0.0) + jnp.where(two, score_two / both, 0.0)
        high = gates.astype(BF16).astype(F32)
        low = gates - high
        table[:, :width] = x[...]
        table[:, width : width + LANES] = (high + pltpu.roll(low, LANES // 2, 1)).astype(BF16)
        table[:, width + LANES :] = cot[...]
        total[...] = jnp.zeros_like(total)

    @pl.when(step < meta[offset + 2 * tiles])
    def _():
        expert = meta[offset + step]
        base = meta[offset + tiles + step]
        row = lax.broadcasted_iota(I32, (TILE, x.shape[0]), 0) + base
        hit = jnp.where(place[0, pl.ds(expert, 1), :] == row, 1.0, 0.0).astype(BF16)
        gathered = dot(hit, table[...])
        inputs = gathered[:, :width].astype(BF16)
        lane = lax.broadcasted_iota(I32, (TILE, LANES), 1)
        mine = (lane == expert) | (lane == expert + LANES // 2)
        scale = jnp.sum(
            jnp.where(mine, gathered[:, width : width + LANES], 0.0), axis=1, keepdims=True
        )
        upstream = gathered[:, width + LANES :]
        both = dot(inputs, w_up[0])
        gate, up = both[:, :hidden_width], both[:, hidden_width:]
        sigma = 1.0 / (1.0 + jnp.exp(-gate))
        active = gate * sigma
        hidden = (active * up).astype(BF16)
        outputs = dot(hidden, w_down[0])
        gate_term = jnp.sum(upstream * outputs, axis=1, keepdims=True)
        grad_row = (upstream * scale).astype(BF16)
        grad_hidden = dot_nt(grad_row, w_down[0])
        grad_gate = (grad_hidden * up * sigma * (1.0 + gate * (1.0 - sigma))).astype(BF16)
        grad_up = (grad_hidden * active).astype(BF16)
        grad_both = jnp.concatenate([grad_gate, grad_up], axis=1)
        grad_x = dot_nt(grad_both, w_up[0])
        x_rows[...] = inputs
        hidden_rows[...] = hidden
        grad_rows[...] = grad_row
        both_rows[...] = grad_both
        back = jnp.concatenate(
            [
                (outputs * scale).astype(BF16),
                grad_x.astype(BF16),
                jnp.where(lane == expert, gate_term, 0.0).astype(BF16),
            ],
            axis=1,
        )
        total[...] += dot_tn(hit, back)

    @pl.when(step == tiles - 1)
    def _():
        rows = x.shape[0]
        feed[...] = total[:, :width].astype(BF16)
        part[:rows, :] = total[:, width : 2 * width].astype(BF16)
        terms = total[:, 2 * width :].T[:16]
        part[rows:, :] = jnp.concatenate(
            [terms, jnp.zeros((16, width - rows), F32)], axis=1
        ).astype(BF16)


def expert_chunk(meta, chunk, x, cot, place, carry, routes, w_router, w_up, w_down, saved):
    rows, width = x.shape
    chunks = place.shape[0]
    hidden_width = w_down.shape[1]
    tiles = most_tiles(rows)
    span = 2 * tiles + 1
    shape = jax.ShapeDtypeStruct
    whole = lambda *dims: pl.BlockSpec(dims, lambda i, m, c: (0,) * len(dims))
    mine = lambda *dims: pl.BlockSpec((1, *dims), lambda i, m, c: (c[0], 0, 0))
    weight = lambda *dims: pl.BlockSpec((1, *dims), lambda i, m, c: (m[c[0] * span + i], 0, 0))

    def kept(columns):
        def index(i, m, c):
            last = jnp.maximum(m[c[0] * span + 2 * tiles] - 1, 0)
            return (c[0] * tiles + jnp.minimum(i, last), 0)

        return pl.BlockSpec((TILE, columns), index)

    columns = (width, hidden_width, width, 2 * hidden_width)
    extra = () if saved is None else tuple(saved)
    return pl.pallas_call(
        functools.partial(expert_kernel, tiles, span),
        grid_spec=pltpu.PrefetchScalarGridSpec(
            num_scalar_prefetch=2,
            grid=(tiles,),
            in_specs=[
                whole(rows, width),
                whole(rows, width),
                mine(8, rows),
                mine(rows, LANES),
                mine(rows, 2),
                whole(width, LANES),
                weight(width, 2 * hidden_width),
                weight(hidden_width, width),
                *[pl.BlockSpec(memory_space=pl.ANY)] * len(extra),
            ],
            out_specs=[
                whole(rows + 16, width),
                whole(rows, width),
                *[kept(c) for c in columns],
            ],
            scratch_shapes=[
                pltpu.VMEM((rows, 2 * width + LANES), BF16),
                pltpu.VMEM((rows, 2 * width + LANES), F32),
            ],
        ),
        out_shape=[
            shape((rows + 16, width), BF16),
            shape((rows, width), BF16),
            *[shape((chunks * tiles * TILE, c), BF16) for c in columns],
        ],
        input_output_aliases={10 + k: 2 + k for k in range(len(extra))},
        compiler_params=pltpu.CompilerParams(vmem_limit_bytes=48 * 2**20),
        cost_estimate=pl.CostEstimate(
            flops=8 * 10**9, bytes_accessed=24 * 2**20, transcendentals=TILE * tiles * hidden_width
        ),
        name="expert_chunk",
    )(meta, chunk, x, cot, place, carry, routes, w_router, w_up, w_down, *extra)


def weight_grad_kernel(steps, walk, x_rows, hidden_rows, grad_rows, both_rows, grad_up, grad_down, sum_up, sum_down):
    step = pl.program_id(0)
    number = walk[2 * steps]
    expert = walk[step]

    @pl.when(step < number)
    def _():
        fresh = (step == 0) | (walk[jnp.maximum(step - 1, 0)] != expert)
        up = dot_tn(x_rows[...], both_rows[...])
        down = dot_tn(hidden_rows[...], grad_rows[...])

        @pl.when(fresh)
        def _():
            sum_up[...] = up
            sum_down[...] = down

        @pl.when(jnp.logical_not(fresh))
        def _():
            sum_up[...] += up
            sum_down[...] += down

        done = (step == number - 1) | (walk[jnp.minimum(step + 1, steps - 1)] != expert)

        @pl.when(done)
        def _():
            grad_up[0] = sum_up[...].astype(BF16)
            grad_down[0] = sum_down[...].astype(BF16)


def weight_grads(walk, saved):
    width, hidden_width = saved[0].shape[1], saved[1].shape[1]
    steps = saved[0].shape[0] // TILE
    shape = jax.ShapeDtypeStruct
    rows = lambda columns: pl.BlockSpec((TILE, columns), lambda i, w: (w[steps + i], 0))
    out = lambda *dims: pl.BlockSpec((1, *dims), lambda i, w: (w[i], 0, 0))
    return pl.pallas_call(
        functools.partial(weight_grad_kernel, steps),
        grid_spec=pltpu.PrefetchScalarGridSpec(
            num_scalar_prefetch=1,
            grid=(steps,),
            in_specs=[rows(kept.shape[1]) for kept in saved],
            out_specs=[out(width, 2 * hidden_width), out(hidden_width, width)],
            scratch_shapes=[
                pltpu.VMEM((width, 2 * hidden_width), F32),
                pltpu.VMEM((hidden_width, width), F32),
            ],
        ),
        out_shape=[
            shape((EXP_FFN, width, 2 * hidden_width), BF16),
            shape((EXP_FFN, hidden_width, width), BF16),
        ],
        compiler_params=pltpu.CompilerParams(vmem_limit_bytes=48 * 2**20),
        cost_estimate=pl.CostEstimate(
            flops=12 * 10**9, bytes_accessed=32 * 2**20, transcendentals=0
        ),
        name="weight_grads",
    )(walk, *saved)


def shards(
    dp_size,
    stream,
    cotangent,
    gain_attention,
    w_inputs,
    w_output,
    gain_experts,
    w_router,
    w_carry,
    w_gate_up,
    w_down,
    w_constant,
    constant_vectors,
    previous_logits,
    routes,
    valid,
    prefix,
):
    rows, width = stream.shape
    tokens = routes.shape[0]
    chunks = tokens // rows
    head_columns = w_inputs.shape[2]
    here = lax.axis_index("tensor")
    index = lax.axis_index("dp")
    outer = (here == 0) | (here == chunks - 1)
    bits = list(range(dp_size.bit_length() - 1))
    first_row = here * rows
    valid_all = valid.astype(F32)
    cut = lambda array, at: lax.dynamic_slice_in_dim(array, at, rows, 0)
    valid_here = cut(valid_all, first_row)
    routes_here = cut(routes, first_row)
    previous_here = cut(previous_logits, first_row)

    w_in_rows = w_inputs.transpose(0, 2, 1)
    packed = jnp.concatenate([w_in_rows, w_output[None]], axis=0).reshape(-1, width)
    piece_rows = packed.shape[0] // dp_size
    piece = lax.dynamic_slice_in_dim(packed, index * piece_rows, piece_rows, 0)
    normed_here, inverse_one = norm_forward(stream, gain_attention)
    normed_low = normed_here.astype(BF16)
    normed_other = along_z(normed_low, SIDE)
    piece = along_z(piece, CROSS)
    partner = spread_blocks(piece, bits[::-1], index, dp_size).reshape(4, head_columns, width)
    both_in = jnp.concatenate([w_in_rows, partner[:3]], axis=1)
    both_out = jnp.concatenate([w_output, partner[3]], axis=0)

    cot_low = cotangent.astype(BF16)
    cot_slots = gather_rows(cot_low, outer)

    place, meta, walk = expert_plan(routes, valid, chunks)
    w_up = w_gate_up.reshape(EXP_FFN, width, -1)
    carry = jnp.dot(previous_logits, w_carry, precision=HIGHEST, preferred_element_type=F32)
    columns = carry.shape[1]
    carry_wide = jnp.pad(carry, ((0, 0), (0, LANES - columns))).reshape(chunks, rows, LANES)
    routes_live = jnp.where(valid[:, None] > 0, routes, -1).reshape(chunks, rows, 2)
    router_wide = jnp.pad(w_router, ((0, 0), (0, LANES - columns)))

    offset = (here % 2) * rows
    sequence = here // 2
    scalars = jnp.stack([offset, prefix[sequence]]).astype(I32)
    cosine, sine = rope_tables(offset)
    valid_rows = jnp.concatenate([cut(valid, first_row), cut(valid, (here ^ 1) * rows)])[:, None]
    fixed = (both_in, both_out, cosine, sine, valid_rows)
    part_own, part_other, *saved_attention = attention_forward(
        scalars, normed_low, normed_other, *fixed
    )
    attention = part_own.astype(F32) + along_z(part_other, SIDE).astype(F32)
    middle = stream + attention
    second, inverse_two = norm_forward(middle, gain_experts)
    second_low = second.astype(BF16)
    second_slots = gather_rows(second_low, outer)

    which = slot_chunks(here)
    saved, parts, feeds = None, [], []
    for slot in range(chunks):
        part, feed, *saved = expert_chunk(
            meta,
            which[slot : slot + 1],
            second_slots[slot],
            cot_slots[slot],
            place,
            carry_wide,
            routes_live,
            router_wide,
            w_up,
            w_down,
            saved,
        )
        parts.append(part)
        feeds.append(feed)
    grad_up, grad_down = weight_grads(walk, saved)

    logits = dot(second_low, w_router) + cut(carry, first_row)
    picked = routes_here[:, :, None] == jnp.arange(columns, dtype=I32)[None, None, :]
    chosen = jnp.sum(jnp.where(picked, logits[:, None, :], 0.0), axis=-1)
    gates_here = jax.nn.softmax(chosen, axis=-1)
    live_gates = gates_here * valid_here[:, None]
    copy_gate = jnp.sum(jnp.where(routes_here == EXP_FFN + 1, live_gates, 0.0), axis=-1)
    constant_gates = jnp.stack(
        [
            jnp.sum(jnp.where(routes_here == EXP_FFN + 2 + number, live_gates, 0.0), axis=-1)
            for number in range(2)
        ],
        axis=1,
    )
    alphas = jax.nn.softmax(
        jnp.einsum("td,cad->tca", second, w_constant, precision=HIGHEST, preferred_element_type=F32),
        axis=-1,
    )
    constant_out = (
        alphas[:, :, 0:1] * second[:, None, :] + alphas[:, :, 1:2] * constant_vectors[None, :, :]
    )
    extra = copy_gate[:, None] * second + jnp.sum(
        constant_gates[:, :, None] * constant_out, axis=1
    )
    copy_terms = jnp.sum(cotangent * second, axis=-1)
    constant_terms = jnp.sum(cotangent[:, None, :] * constant_out, axis=-1)
    grad_constant_out = constant_gates[:, :, None] * cotangent[:, None, :]
    grad_vectors = jnp.sum(alphas[:, :, 1:2] * grad_constant_out, axis=0)
    grad_alphas = jnp.stack(
        [
            jnp.sum(grad_constant_out * second[:, None, :], axis=-1),
            jnp.sum(grad_constant_out * constant_vectors[None, :, :], axis=-1),
        ],
        axis=-1,
    )
    grad_mix = alphas * (grad_alphas - jnp.sum(alphas * grad_alphas, axis=-1, keepdims=True))
    grad_constant = jnp.einsum(
        "tca,td->cad", grad_mix, second, precision=HIGHEST, preferred_element_type=F32
    )
    grad_local = (
        copy_gate[:, None] * cotangent
        + jnp.sum(alphas[:, :, 0:1] * grad_constant_out, axis=1)
        + jnp.einsum(
            "tca,cad->td", grad_mix, w_constant, precision=HIGHEST, preferred_element_type=F32
        )
    )

    summed = scatter_rows(parts)
    gate_grads = summed[rows : rows + EXP_FFN, :rows].T
    gate_table = jnp.concatenate(
        [gate_grads, jnp.zeros((rows, 1), F32), copy_terms[:, None], constant_terms], axis=1
    )
    grad_gates = jnp.sum(jnp.where(picked, gate_table[:, None, :], 0.0), axis=-1)
    grad_gates = grad_gates * valid_here[:, None]
    grad_chosen = gates_here * (
        grad_gates - jnp.sum(gates_here * grad_gates, axis=-1, keepdims=True)
    )
    grad_logits = jnp.sum(jnp.where(picked, grad_chosen[:, :, None], 0.0), axis=1)
    grad_router = jnp.dot(
        second_low.astype(F32).T, grad_logits, precision=HIGHEST, preferred_element_type=F32
    )
    grad_carry = jnp.dot(
        previous_here.T, grad_logits, precision=HIGHEST, preferred_element_type=F32
    )
    grad_previous = jnp.dot(
        grad_logits, w_carry.T, precision=HIGHEST, preferred_element_type=F32
    )
    grad_second = (
        summed[:rows]
        + grad_local
        + jnp.dot(
            grad_logits, w_router.astype(F32).T, precision=HIGHEST, preferred_element_type=F32
        )
    )
    grad_gain_experts = jnp.sum(grad_second * middle * inverse_two, axis=0)
    grad_middle = cotangent + norm_backward(middle, inverse_two, gain_experts, grad_second)

    grad_low = grad_middle.astype(BF16)
    grad_other = along_z(grad_low, SIDE)
    part_own, part_other, grad_w, grad_o, gain_rows = attention_backward(
        scalars, normed_low, normed_other, *fixed, grad_low, grad_other, saved_attention
    )
    grad_normed = part_own.astype(F32) + along_z(part_other, SIDE).astype(F32)
    grad_stream = grad_middle + norm_backward(stream, inverse_one, gain_attention, grad_normed)

    feed = scatter_rows(feeds)
    experts = feed + extra
    block_out = middle + experts
    squares = [
        jnp.sum(valid_here[:, None] * part * part) for part in (block_out, attention, experts)
    ]
    squares = jnp.stack([*squares, jnp.sum(valid_here)])

    rotated = [bits[0], *bits[:0:-1]]
    cut_up = jnp.split(grad_up.reshape(-1, grad_up.shape[2]), 2, axis=0)
    cut_down = jnp.split(grad_down.reshape(-1, width), 2, axis=0)
    done = []
    for halves in (cut_up, cut_down):
        both = []
        for half, order in zip(halves, (bits, rotated)):
            reduced = reduce_blocks(half, order, index, dp_size)
            both.append(spread_blocks(reduced, order, index, dp_size))
        done.append(jnp.concatenate(both, axis=0).astype(F32))
    grad_gate_up = done[0].reshape(EXP_FFN, width, 2, -1)
    grad_down = done[1].reshape(EXP_FFN, -1, width)

    own_grads = jnp.concatenate([grad_w[:, :head_columns], grad_o[None, :head_columns]], axis=0)
    far_grads = jnp.concatenate([grad_w[:, head_columns:], grad_o[None, head_columns:]], axis=0)
    order = bits[::-1]
    own_piece = reduce_blocks(own_grads.reshape(-1, width), order, index, dp_size)
    far_piece = reduce_blocks(far_grads.reshape(-1, width), order, index, dp_size)
    own_piece = own_piece + along_z(far_piece, CROSS)
    attention_grads = spread_blocks(own_piece, order, index, dp_size).astype(F32)
    attention_grads = attention_grads.reshape(4, head_columns, width)
    grad_inputs = attention_grads[:3].transpose(0, 2, 1)
    grad_output = attention_grads[3]

    wide = lambda array: jnp.pad(array, ((0, 0), (0, width - array.shape[1])))
    small = jnp.concatenate(
        [
            grad_gain_experts[None],
            grad_router.T,
            wide(grad_carry),
            grad_constant.reshape(-1, width),
            grad_vectors,
            wide(squares[None]),
        ],
        axis=0,
    )
    small = sum_everywhere(small, bits, dp_size)
    gain_row = jnp.sum(gain_rows, axis=0, keepdims=True) / gain_attention[None]
    gain_row = sum_everywhere(gain_row, bits, dp_size)
    at = 1 + 2 * columns
    squares = small[at + 6, :3]
    counted = small[at + 6, 3]
    rms_values = jnp.sqrt(squares / (jnp.maximum(counted, 1.0) * width))
    return (
        block_out,
        grad_stream,
        gain_row[0],
        grad_inputs,
        grad_output,
        small[0],
        small[1 : 1 + columns].T,
        small[1 + columns : at, :columns],
        grad_gate_up,
        grad_down,
        small[at : at + 4].reshape(2, 2, width),
        small[at + 4 : at + 6],
        grad_previous,
        rms_values,
    )


def solution(mesh):
    return jax.shard_map(
        functools.partial(shards, mesh.shape["dp"]),
        mesh=mesh,
        in_specs=(
            P(("dp", "tensor"), None),
            P(("dp", "tensor"), None),
            P(),
            P(None, None, "tensor"),
            P("tensor", None),
            P(),
            P(),
            P(),
            P(None, None, None, "tensor"),
            P(None, "tensor", None),
            P(),
            P(),
            P("dp", None),
            P("dp", None),
            P("dp"),
            P("dp"),
        ),
        out_specs=(
            P(("dp", "tensor"), None),
            P(("dp", "tensor"), None),
            P(),
            P(None, None, "tensor"),
            P("tensor", None),
            P(),
            P(),
            P(),
            P(None, None, None, "tensor"),
            P(None, "tensor", None),
            P(),
            P(),
            P(("dp", "tensor"), None),
            P(),
        ),
        check_vma=False,
    )
```

time: 1220 us -> 723 us (0.59)
  matrix products: 328 us -> 7.73 us
  waiting for transfers between devices: 402 us -> 186 us
  Pallas kernels: 0 us -> 191 us
  starting transfers between devices: 0.42 us -> 149 us
  local copies, waits for them, and re-layouts: 228 us -> 87.3 us
  other arithmetic: 186 us -> 92.2 us
  blocking collectives: 43.2 us -> 0 us
  between operations: 16.9 us -> 4.37 us
    dot_general x42 -> x4, matrix products: 317 us -> 1.79 us  [the longest x1 0.83 us: shards(): jnp.dot(grad_logits, w_router.astype(F32).T, precision=HIGHEST, preferred...]
    pallas_call x0 -> x7, Pallas kernels: none -> 191 us  [the longest x4 77.4 us: expert_chunk(): pl.pallas_call(functools.partial(expert_kernel, tiles, span), grid_spec=p...]
    ppermute x0 -> x72, waiting for transfers between devices: none -> 186 us  [the longest x42 112 us: along_dp(): return lax.ppermute(value, 'dp', [(i, i ^ 1 << bit) for i in range(size)])]
    ppermute x0 -> x72, starting transfers between devices: none -> 149 us  [the longest x30 76.2 us: along_z(): return lax.ppermute(value, 'tensor', pairs)]
    all_gather x4 -> x0, waiting for transfers between devices: 147 us -> none  [the longest x1 64.5 us: shards(): lax.all_gather(normed_here.astype(jnp.bfloat16), 'tensor', axis=0, tiled=...]
    gather x12 -> x0, local copies, waits for them, and re-layouts: 143 us -> none  [the longest x3 38.9 us: expert_slots(): live = jnp.take_along_axis(used.T, order, axis=1)]
    psum x1 -> x0, waiting for transfers between devices: 130 us -> none  [shards(): lax.psum(grad_gate_up.astype(jnp.bfloat16), 'dp').astype(jnp.float32)]
    reduce_scatter x5 -> x0, waiting for transfers between devices: 124 us -> none  [the longest x1 53.8 us: shards(): lax.psum_scatter(jnp.dot(mixed, w_output, preferred_element_type=jnp.floa...]
  transfers between devices with their start and end apart: 10 -> 72, of which waited for: 7 -> 27; matrix products, arithmetic and copies ran while one was open for 22% -> 19% of each run, Pallas kernels for 0% -> 13%
where the time goes in v1:
time: 723 us; the launch traced here: 717 us
  Pallas kernels  191 us (26%)
  waiting for transfers between devices  186 us (26%)
  starting transfers between devices  149 us (21%)
  other arithmetic  92.2 us (13%)
  local copies, waits for them, and re-layouts  87.3 us (12%)
  matrix products  7.73 us (1%)
    ppermute x42, waiting for transfers between devices, along_dp(): return lax.ppermute(value, 'dp', [(i, i ^ 1 << bit) for i in range(size)])  112 us
    pallas_call x4, Pallas kernels, expert_chunk(): pl.pallas_call(functools.partial(expert_kernel, tiles, span), grid_spec=p...  77.4 us
    ppermute x30, starting transfers between devices, along_z(): return lax.ppermute(value, 'tensor', pairs)  76.2 us
    ppermute x30, waiting for transfers between devices, along_z(): return lax.ppermute(value, 'tensor', pairs)  73.3 us
    ppermute x42, starting transfers between devices, along_dp(): return lax.ppermute(value, 'dp', [(i, i ^ 1 << bit) for i in range(size)])  72.5 us
    pallas_call x1, Pallas kernels, weight_grads(): pl.pallas_call(functools.partial(weight_grad_kernel, steps), grid_spec=pl...  40.3 us
    pallas_call x1, Pallas kernels, attention_backward(): pl.pallas_call(attention_back_kernel, grid_spec=pltpu.PrefetchScalarGridS...  37.9 us
    pallas_call x1, Pallas kernels, attention_forward(): pl.pallas_call(attention_kernel, grid_spec=pltpu.PrefetchScalarGridSpec(n...  35.5 us
  transfers between devices with their start and end apart: 72, of which 27 were waited for; matrix products, arithmetic and copies ran while one was open for 19% of the time, Pallas kernels for 13%

profile of v1, /device:TPU:0, one launch (start us, length us, event | category | flops | bytes accessed | tf_op | source)
XLA Modules:
  0.0 717.0 jit_solution(3789346032114522750)
XLA Ops:
  2.2 4.1 collective-permute-start.1
  17.4 1.9 fusion.18
  19.3 5.0 collective-permute-done.3
  30.7 9.6 %collective-permute-done.4 = bf16[384,768]{1,0:T(8,128)(2,1)} collective-permute-done((bf16[384,768]{1,0:T(8,128)(2,1)S(1)}, bf16[384,768]{1,0:T(8,128)(2,1)}, u32[]{:S(2)}, u32[]{:S(2)}) %collective-permute-start.4) | collective-permute-done | bytes 589856 | tf_op jit(solution)/shard_map/ppermute | solution.py:58
  44.5 35.5 %attention_forward.1 = (bf16[512,768]{1,0:T(8,128)(2,1)S(1)}, bf16[512,768]{1,0:T(8,128)(2,1)}, bf16[1024,384]{1,0:T(8,128)(2,1)S(1)}, bf16[1024,384]{1,0:T(8,12...) custom-call(s32[2]{0:T(128)S(1)} %pad_add_fusion.2.scalars, ...), custom_call_target="tpu_custom_call" | custom-call | flops 5637144576 | bytes 12582912 | tf_op jit(solution)/shard_map/attention_forward/pallas_call | solution.py:218
  83.5 15.9 %reshape.437.w_up = bf16[6,768,1024]{2,1,0:T(8,128)(2,1)} reshape(bf16[6,768,2,512]{3,2,1,0:T(2,128)(2,1)} %param.25) | data formatting | bytes 18874368 | tf_op jit(solution)/shard_map/reshape | solution.py:648
  105.8 2.1 multiply_reduce_fusion.6
  108.6 1.9 multiply_reduce_fusion.5
  113.7 2.9 collective-permute-start.11
  120.0 19.3 %expert_chunk.4 = (bf16[528,768]{1,0:T(8,128)(2,1)S(1)}, bf16[512,768]{1,0:T(8,128)(2,1)S(1)}, bf16[6656,768]{1,0:T(8,128)(2,1)}, bf16[6656,512]{1,0:T(8,128)(2,...) custom-call(s32[108]{0:T(128)S(1)} %reshape.433.meta, s32[1]{0:T(128)} %bitcast.7.chunk, ...), custom_call_target="tpu_custom_call" | custom-call | flops 8000000000 | bytes 25165824 | tf_op jit(solution)/shard_map/expert_chunk/pallas_call | solution.py:499
  144.5 2.3 collective-permute-done.11.cot
  147.5 20.0 %expert_chunk.5 = (bf16[528,768]{1,0:T(8,128)(2,1)S(1)}, bf16[512,768]{1,0:T(8,128)(2,1)S(1)}, bf16[6656,768]{1,0:T(8,128)(2,1)}, bf16[6656,512]{1,0:T(8,128)(2,...) custom-call(s32[108]{0:T(128)S(1)} %reshape.433.meta, ...), custom_call_target="tpu_custom_call", output_to_operand_aliasing={{2}: (10, {}), {3}: (11, {}), {4}: (12, {}), {5}: (13, {})} | custom-call | flops 8000000000 | bytes 25165824 | tf_op jit(solution)/shard_map/expert_chunk/pallas_call | solution.py:499
  168.9 11.6 %collective-permute-done.9 = bf16[512,768]{1,0:T(8,128)(2,1)S(1)} collective-permute-done((bf16[512,768]{1,0:T(8,128)(2,1)}, bf16[512,768]{1,0:T(8,128)(2,1)S(1)}, u32[]{:S(2)}, u32[]{:S(2)}) %collective-permute-start.9) | collective-permute-done | bytes 786464 | tf_op jit(solution)/shard_map/ppermute | solution.py:54
  181.9 19.0 %expert_chunk.6 = (bf16[528,768]{1,0:T(8,128)(2,1)S(1)}, bf16[512,768]{1,0:T(8,128)(2,1)S(1)}, bf16[6656,768]{1,0:T(8,128)(2,1)}, bf16[6656,512]{1,0:T(8,128)(2,...) custom-call(s32[108]{0:T(128)S(1)} %reshape.433.meta, ...), custom_call_target="tpu_custom_call", output_to_operand_aliasing={{2}: (10, {}), {3}: (11, {}), {4}: (12, {}), {5}: (13, {})} | custom-call | flops 8000000000 | bytes 25165824 | tf_op jit(solution)/shard_map/expert_chunk/pallas_call | solution.py:499
  201.1 11.4 %collective-permute-done.17 = bf16[512,768]{1,0:T(8,128)(2,1)S(1)} collective-permute-done((bf16[512,768]{1,0:T(8,128)(2,1)S(1)}, bf16[512,768]{1,0:T(8,128)(2,1)S(1)}, u32[]{:S(2)}, u32[]{:S(2)}) %collective-permute-start.17) | collective-permute-done | bytes 786464 | tf_op jit(solution)/shard_map/ppermute | solution.py:54
  212.5 19.0 %expert_chunk.7 = (bf16[528,768]{1,0:T(8,128)(2,1)S(1)}, bf16[512,768]{1,0:T(8,128)(2,1)S(1)}, bf16[6656,768]{1,0:T(8,128)(2,1)}, bf16[6656,512]{1,0:T(8,128)(2,...) custom-call(s32[108]{0:T(128)S(1)} %reshape.433.meta, ...), custom_call_target="tpu_custom_call", output_to_operand_aliasing={{2}: (10, {}), {3}: (11, {}), {4}: (12, {}), {5}: (13, {})} | custom-call | flops 8000000000 | bytes 25165824 | tf_op jit(solution)/shard_map/expert_chunk/pallas_call | solution.py:499
  233.4 40.3 %weight_grads.1 = (bf16[6,768,1024]{2,1,0:T(8,128)(2,1)}, bf16[6,512,768]{2,1,0:T(8,128)(2,1)S(1)}) custom-call(s32[105]{0:T(128)S(1)} %pad_add_fusion.3.walk, bf16[6656,768]{1,0:T(8,128)(2,1)} %get-tuple-element.84.x_rows, bf16[6656,512]{1,0:T(8,128)(2,1)} %get-tuple-element.85.hidden_rows, bf16[6656,768]{1,0:T(8,128)(2,1)} %get-tuple-element.86.grad_rows, ...), custom_call_target="tpu_custom_call" | custom-call | flops 12000000000 | bytes 33554432 | tf_op jit(solution)/shard_map/weight_grads/pallas_call | solution.py:574
  278.3 4.5 fusion.2
  284.3 2.3 collective-permute-start.12
  288.0 2.5 collective-permute-start.23
  290.5 1.9 dynamic-slice_add_fusion.3
  297.4 7.0 collective-permute-start.67
  304.4 7.2 %fusion.50 = (bf16[3,768,1024]{2,1,0:T(8,128)(2,1)}, bf16[3,768,1024]{2,1,0:T(8,128)(2,1)S(1)}) fusion(bf16[6,768,1024]{2,1,0:T(8,128)(2,1)} %get-tuple-element.88), kind=kLoop, calls=%fused_computation.231 | loop fusion | bytes 18874368 | tf_op jit(solution)/shard_map/split | solution.py:783
  311.6 25.9 %collective-permute-done.23 = bf16[528,768]{1,0:T(8,128)(2,1)} collective-permute-done((bf16[528,768]{1,0:T(8,128)(2,1)S(1)}, bf16[528,768]{1,0:T(8,128)(2,1)}, u32[]{:S(2)}, u32[]{:S(2)}) %collective-permute-start.23) | collective-permute-done | bytes 811040 | tf_op jit(solution)/shard_map/ppermute | solution.py:54
  337.5 4.5 collective-permute-start.18
  348.5 7.8 %collective-permute-start.68 = (bf16[192,768]{1,0:T(8,128)(2,1)S(1)}, bf16[192,768]{1,0:T(8,128)(2,1)S(1)}, u32[]{:S(2)}, u32[]{:S(2)}) collective-permute-start(bf16[192,768]{1,0:T(8,128)(2,1)S(1)} %constant_dynamic-slice_fusion), channel_id=1, source_target_pairs={{0,8},{4,12},{8,0},{12,4},{16,24},{20,28},{24,16},{28,20},{1,9},{5... | collective-permute-start | bytes 884744 | tf_op jit(solution)/shard_map/ppermute | solution.py:58
  361.5 6.7 collective-permute-start.25
  368.5 7.0 collective-permute-start.69
  381.3 23.7 %collective-permute-start.20 = (bf16[512,768]{1,0:T(8,128)(2,1)S(1)}, bf16[512,768]{1,0:T(8,128)(2,1)S(1)}, u32[]{:S(2)}, u32[]{:S(2)}) collective-permute-start(bf16[512,768]{1,0:T(8,128)(2,1)S(1)} %add.407), channel_id=1, source_target_pairs={{0,1},{1,0},{2,3},{3,2},{4,5},{5,4},{6,7},{7,6},{8,9},{9,8},{10,11... | collective-permute-start | bytes 2359304 | tf_op jit(solution)/shard_map/ppermute | solution.py:54
  409.0 2.4 multiply_reduce_fusion.2
  411.4 8.0 %collective-permute-start.70 = (bf16[384,768]{1,0:T(8,128)(2,1)}, bf16[384,768]{1,0:T(8,128)(2,1)}, u32[]{:S(2)}, u32[]{:S(2)}) collective-permute-start(bf16[384,768]{1,0:T(8,128)(2,1)} %maximum_select_fusion.15), channel_id=1, source_target_pairs={{0,16},{4,20},{8,24},{12,28},{16,0},{20,4},{24,8},{28,12},{1,17},{... | collective-permute-start | bytes 1769480 | tf_op jit(solution)/shard_map/ppermute | solution.py:58
  419.5 3.3 collective-permute-done.20
  422.8 5.0 fusion.47
  427.8 2.7 maximum_bitcast_fusion
  431.6 3.5 dynamic-slice_add_fusion.1
  438.4 2.0 collective-permute-done.44
  440.4 7.8 %collective-permute-start.45 = (f32[28,768]{1,0:T(8,128)S(1)}, f32[28,768]{1,0:T(8,128)S(1)}, u32[]{:S(2)}, u32[]{:S(2)}) collective-permute-start(f32[28,768]{1,0:T(8,128)S(1)} %add.445), channel_id=1, source_target_pairs={{0,16},{4,20},{8,24},{12,28},{16,0},{20,4},{24,8},{28,12},{1,17},{... | collective-permute-start | bytes 258056 | tf_op jit(solution)/shard_map/ppermute | solution.py:58
  448.2 2.8 dynamic-slice_add_fusion
  458.2 3.3 collective-permute-done.47
  468.0 3.0 maximum_select_fusion.10
  471.1 3.1 maximum_select_fusion.11
  474.6 3.9 collective-permute-done.26.grad_other
  479.5 37.9 %attention_backward.1 = (bf16[512,768]{1,0:T(8,128)(2,1)S(1)}, bf16[512,768]{1,0:T(8,128)(2,1)S(1)}, bf16[3,384,768]{2,1,0:T(8,128)(2,1)}, bf16[384,768]{1,0:T(8,128)(2,1)S(1)}, f32[8,768]{1,0:T(8,128)S(1)}) custom-call(s32[2]{0:T(128)S(1)} %pad_add_fusion.2.scalars, bf16[512,768]{1,0:T(8,128)(2,1)S(1)} %copy-done.12, ...), custom_call_target="tpu_custom_call" | custom-call | flops 12884901888 | bytes 20971520 | tf_op jit(solution)/shard_map/attention_backward/pallas_call | solution.py:319
  517.4 2.5 fusion.52
  526.4 1.9 collective-permute-done.30
  533.6 2.8 collective-permute-done.32
  544.2 8.5 %collective-permute-done.33 = bf16[384,768]{1,0:T(8,128)(2,1)S(1)} collective-permute-done((bf16[384,768]{1,0:T(8,128)(2,1)S(1)}, bf16[384,768]{1,0:T(8,128)(2,1)S(1)}, u32[]{:S(2)}, u32[]{:S(2)}) %collective-permute-start.33) | collective-permute-done | bytes 589856 | tf_op jit(solution)/shard_map/ppermute | solution.py:58
  554.5 10.9 %collective-permute-done.36 = bf16[384,768]{1,0:T(8,128)(2,1)S(1)} collective-permute-done((bf16[384,768]{1,0:T(8,128)(2,1)S(1)}, bf16[384,768]{1,0:T(8,128)(2,1)S(1)}, u32[]{:S(2)}, u32[]{:S(2)}) %collective-permute-start.36) | collective-permute-done | bytes 589856 | tf_op jit(solution)/shard_map/ppermute | solution.py:58
  567.3 7.4 %collective-permute-done.50 = bf16[288,1024]{1,0:T(8,128)(2,1)S(1)} collective-permute-done((bf16[288,1024]{1,0:T(8,128)(2,1)S(1)}, bf16[288,1024]{1,0:T(8,128)(2,1)S(1)}, u32[]{:S(2)}, u32[]{:S(2)}) %collective-permute-start.50) | collective-permute-done | bytes 589856 | tf_op jit(solution)/shard_map/ppermute | solution.py:58
  576.8 2.1 collective-permute-start.37
  580.9 4.4 collective-permute-done.51
  589.0 10.5 %collective-permute-done.57 = bf16[288,1024]{1,0:T(8,128)(2,1)S(1)} collective-permute-done((bf16[288,1024]{1,0:T(8,128)(2,1)S(1)}, bf16[288,1024]{1,0:T(8,128)(2,1)S(1)}, u32[]{:S(2)}, u32[]{:S(2)}) %collective-permute-start.57) | collective-permute-done | bytes 589856 | tf_op jit(solution)/shard_map/ppermute | solution.py:58
  600.1 25.7 %collective-permute-done.34 = bf16[192,768]{1,0:T(8,128)(2,1)S(1)} collective-permute-done((bf16[192,768]{1,0:T(8,128)(2,1)S(1)}, bf16[192,768]{1,0:T(8,128)(2,1)S(1)}, u32[]{:S(2)}, u32[]{:S(2)}) %collective-permute-start.34) | collective-permute-done | bytes 294944 | tf_op jit(solution)/shard_map/ppermute | solution.py:58
  631.0 7.0 collective-permute-done.39
  638.2 11.0 %collective-permute-done.58 = bf16[576,1024]{1,0:T(8,128)(2,1)S(1)} collective-permute-done((bf16[576,1024]{1,0:T(8,128)(2,1)S(1)}, bf16[576,1024]{1,0:T(8,128)(2,1)S(1)}, u32[]{:S(2)}, u32[]{:S(2)}) %collective-permute-start.58) | collective-permute-done | bytes 1179680 | tf_op jit(solution)/shard_map/ppermute | solution.py:58
  653.8 2.7 maximum_select_fusion.4
  656.6 5.2 collective-permute-done.41
  663.8 2.7 maximum_select_fusion.5
  666.8 4.6 convert.2
  671.4 5.6 collective-permute-done.42
  679.4 2.6 maximum_select_fusion
  682.0 2.9 maximum_select_fusion.1
  684.9 7.0 maximum_convert_fusion
  691.9 24.6 %reshape.442 = f32[6,768,2,512]{3,2,1,0:T(2,128)} reshape(f32[4608,1024]{1,0:T(8,128)} %maximum_convert_fusion) | data formatting | bytes 37748736 | tf_op jit(solution)/shard_map/convert_element_type | solution.py:791
  (478 shorter events, 148.7 us)
Async XLA Ops:
  2.2 11.4 %collective-permute-start.1 = (bf16[96,768]{1,0:T(8,128)(2,1)S(1)}, bf16[96,768]{1,0:T(8,128)(2,1)S(1)}, u32[]{:S(2)}, u32[]{:S(2)}) collective-permute-start(bf16[96,768]{1,0:T(8,128)(2,1)S(1)} %constant_dynamic-slice_fusion.20), channel_id=1, source_target_pairs={{0,2},{1,3},{2,0},{3,1},{4,6},{5,7},{6,4},{7,5},{8,10},{9,11},{10,... | collective-permute-start | bytes 442376 | tf_op jit(solution)/shard_map/ppermute | solution.py:54
  7.3 37.2 %collective-permute-start = (bf16[512,768]{1,0:T(8,128)(2,1)S(1)}, bf16[512,768]{1,0:T(8,128)(2,1)}, u32[]{:S(2)}, u32[]{:S(2)}) collective-permute-start(bf16[512,768]{1,0:T(8,128)(2,1)S(1)} %multiply_convert_fusion.own), channel_id=1, source_target_pairs={{0,1},{1,0},{2,3},{3,2},{4,5},{5,4},{6,7},{7,6},{8,9},{9,8},{10,11... | collective-permute-start | bytes 2359304 | tf_op jit(solution)/shard_map/ppermute | solution.py:54
  15.1 9.2 %collective-permute-start.3 = (bf16[192,768]{1,0:T(8,128)(2,1)S(1)}, bf16[192,768]{1,0:T(8,128)(2,1)}, u32[]{:S(2)}, u32[]{:S(2)}) collective-permute-start(bf16[192,768]{1,0:T(8,128)(2,1)S(1)} %maximum_select_fusion.16), channel_id=1, source_target_pairs={{0,8},{4,12},{8,0},{12,4},{16,24},{20,28},{24,16},{28,20},{1,9},{5... | collective-permute-start | bytes 884744 | tf_op jit(solution)/shard_map/ppermute | solution.py:58
  25.6 14.7 %collective-permute-start.4 = (bf16[384,768]{1,0:T(8,128)(2,1)S(1)}, bf16[384,768]{1,0:T(8,128)(2,1)}, u32[]{:S(2)}, u32[]{:S(2)}) collective-permute-start(bf16[384,768]{1,0:T(8,128)(2,1)S(1)} %maximum_select_fusion.12), channel_id=1, source_target_pairs={{0,16},{4,20},{8,24},{12,28},{16,0},{20,4},{24,8},{28,12},{1,17},{... | collective-permute-start | bytes 1769480 | tf_op jit(solution)/shard_map/ppermute | solution.py:58
  82.7 23.1 %collective-permute-start.5 = (bf16[512,768]{1,0:T(8,128)(2,1)}, bf16[512,768]{1,0:T(8,128)(2,1)}, u32[]{:S(2)}, u32[]{:S(2)}) collective-permute-start(bf16[512,768]{1,0:T(8,128)(2,1)} %get-tuple-element.53), channel_id=1, source_target_pairs={{0,1},{1,0},{2,3},{3,2},{4,5},{5,4},{6,7},{7,6},{8,9},{9,8},{10,11... | collective-permute-start | bytes 2359304 | tf_op jit(solution)/shard_map/ppermute | solution.py:54
  110.5 31.9 %collective-permute-start.10 = (bf16[512,768]{1,0:T(8,128)(2,1)S(1)}, bf16[512,768]{1,0:T(8,128)(2,1)}, u32[]{:S(2)}, u32[]{:S(2)}) collective-permute-start(bf16[512,768]{1,0:T(8,128)(2,1)S(1)} %convert_element_type.108.x), channel_id=1, source_target_pairs={{0,1},{1,0},{2,3},{3,2},{4,5},{5,4},{6,7},{7,6},{8,9},{9,8},{10,11... | collective-permute-start | bytes 2359304 | tf_op jit(solution)/shard_map/ppermute | solution.py:54
  112.2 28.9 %collective-permute-start.6 = (bf16[512,768]{1,0:T(8,128)(2,1)S(1)}, bf16[512,768]{1,0:T(8,128)(2,1)}, u32[]{:S(2)}, u32[]{:S(2)}) collective-permute-start(bf16[512,768]{1,0:T(8,128)(2,1)S(1)} %convert_element_type.108.x), channel_id=1, source_target_pairs={{1,2},{2,1},{5,6},{6,5},{9,10},{10,9},{13,14},{14,13},{17,18},{18,... | collective-permute-start | bytes 2359304 | tf_op jit(solution)/shard_map/ppermute | solution.py:54
  113.7 33.0 %collective-permute-start.11 = (bf16[512,768]{1,0:T(8,128)(2,1)}, bf16[512,768]{1,0:T(8,128)(2,1)}, u32[]{:S(2)}, u32[]{:S(2)}) collective-permute-start(bf16[512,768]{1,0:T(8,128)(2,1)} %get-tuple-element.129.cot), channel_id=1, source_target_pairs={{0,1},{1,0},{2,3},{3,2},{4,5},{5,4},{6,7},{7,6},{8,9},{9,8},{10,11... | collective-permute-start | bytes 2359304 | tf_op jit(solution)/shard_map/ppermute | solution.py:54
  116.6 26.6 %collective-permute-start.8 = (bf16[512,768]{1,0:T(8,128)(2,1)}, bf16[512,768]{1,0:T(8,128)(2,1)}, u32[]{:S(2)}, u32[]{:S(2)}) collective-permute-start(bf16[512,768]{1,0:T(8,128)(2,1)} %get-tuple-element.129.cot), channel_id=1, source_target_pairs={{1,2},{2,1},{5,6},{6,5},{9,10},{10,9},{13,14},{14,13},{17,18},{18,... | collective-permute-start | bytes 2359304 | tf_op jit(solution)/shard_map/ppermute | solution.py:54
  141.1 27.7 %collective-permute-start.7 = (bf16[512,768]{1,0:T(8,128)(2,1)}, bf16[512,768]{1,0:T(8,128)(2,1)S(1)}, u32[]{:S(2)}, u32[]{:S(2)}) collective-permute-start(bf16[512,768]{1,0:T(8,128)(2,1)} %collective-permute-done.6), channel_id=1, source_target_pairs={{1,0},{2,3},{5,4},{6,7},{9,8},{10,11},{13,12},{14,15},{17,16},{18,... | collective-permute-start | bytes 2359304 | tf_op jit(solution)/shard_map/ppermute | solution.py:54
  142.4 25.1 %collective-permute-start.14 = (bf16[512,768]{1,0:T(8,128)(2,1)}, bf16[512,768]{1,0:T(8,128)(2,1)S(1)}, u32[]{:S(2)}, u32[]{:S(2)}) collective-permute-start(bf16[512,768]{1,0:T(8,128)(2,1)} %collective-permute-done.10.x), channel_id=1, source_target_pairs={{1,2},{2,1},{5,6},{6,5},{9,10},{10,9},{13,14},{14,13},{17,18},{18,... | collective-permute-start | bytes 2359304 | tf_op jit(solution)/shard_map/ppermute | solution.py:54
  143.2 37.4 %collective-permute-start.9 = (bf16[512,768]{1,0:T(8,128)(2,1)}, bf16[512,768]{1,0:T(8,128)(2,1)S(1)}, u32[]{:S(2)}, u32[]{:S(2)}) collective-permute-start(bf16[512,768]{1,0:T(8,128)(2,1)} %collective-permute-done.8), channel_id=1, source_target_pairs={{1,0},{2,3},{5,4},{6,7},{9,8},{10,11},{13,12},{14,15},{17,16},{18,... | collective-permute-start | bytes 2359304 | tf_op jit(solution)/shard_map/ppermute | solution.py:54
  146.7 33.9 %collective-permute-start.16 = (bf16[512,768]{1,0:T(8,128)(2,1)}, bf16[512,768]{1,0:T(8,128)(2,1)S(1)}, u32[]{:S(2)}, u32[]{:S(2)}) collective-permute-start(bf16[512,768]{1,0:T(8,128)(2,1)} %collective-permute-done.11.cot), channel_id=1, source_target_pairs={{1,2},{2,1},{5,6},{6,5},{9,10},{10,9},{13,14},{14,13},{17,18},{18,... | collective-permute-start | bytes 2359304 | tf_op jit(solution)/shard_map/ppermute | solution.py:54
  167.5 33.5 %collective-permute-start.15 = (bf16[512,768]{1,0:T(8,128)(2,1)S(1)}, bf16[512,768]{1,0:T(8,128)(2,1)S(1)}, u32[]{:S(2)}, u32[]{:S(2)}) collective-permute-start(bf16[512,768]{1,0:T(8,128)(2,1)S(1)} %collective-permute-done.14), channel_id=1, source_target_pairs={{1,0},{2,3},{5,4},{6,7},{9,8},{10,11},{13,12},{14,15},{17,16},{18,... | collective-permute-start | bytes 2359304 | tf_op jit(solution)/shard_map/ppermute | solution.py:54
  180.6 31.8 %collective-permute-start.17 = (bf16[512,768]{1,0:T(8,128)(2,1)S(1)}, bf16[512,768]{1,0:T(8,128)(2,1)S(1)}, u32[]{:S(2)}, u32[]{:S(2)}) collective-permute-start(bf16[512,768]{1,0:T(8,128)(2,1)S(1)} %collective-permute-done.16), channel_id=1, source_target_pairs={{1,0},{2,3},{5,4},{6,7},{9,8},{10,11},{13,12},{14,15},{17,16},{18,... | collective-permute-start | bytes 2359304 | tf_op jit(solution)/shard_map/ppermute | solution.py:54
  275.1 15.4 %collective-permute-start.60 = (bf16[768,768]{1,0:T(8,128)(2,1)}, bf16[768,768]{1,0:T(8,128)(2,1)}, u32[]{:S(2)}, u32[]{:S(2)}) collective-permute-start(bf16[768,768]{1,0:T(8,128)(2,1)} %constant_dynamic-slice_fusion.5), channel_id=1, source_target_pairs={{0,4},{4,0},{8,12},{12,8},{16,20},{20,16},{24,28},{28,24},{1,5},{5... | collective-permute-start | bytes 3538952 | tf_op jit(solution)/shard_map/ppermute | solution.py:58
  277.6 17.2 %collective-permute-start.66 = (bf16[768,768]{1,0:T(8,128)(2,1)}, bf16[768,768]{1,0:T(8,128)(2,1)}, u32[]{:S(2)}, u32[]{:S(2)}) collective-permute-start(bf16[768,768]{1,0:T(8,128)(2,1)} %constant_dynamic-slice_fusion.2), channel_id=1, source_target_pairs={{0,4},{4,0},{8,12},{12,8},{16,20},{20,16},{24,28},{28,24},{1,5},{5... | collective-permute-start | bytes 3538952 | tf_op jit(solution)/shard_map/ppermute | solution.py:58
  284.3 64.1 %collective-permute-start.12 = (bf16[512,768]{1,0:T(8,128)(2,1)S(1)}, bf16[512,768]{1,0:T(8,128)(2,1)}, u32[]{:S(2)}, u32[]{:S(2)}) collective-permute-start(bf16[512,768]{1,0:T(8,128)(2,1)S(1)} %copy-done.16), channel_id=1, source_target_pairs={{0,1},{3,2},{4,5},{7,6},{8,9},{11,10},{12,13},{15,14},{16,17},{19,... | collective-permute-start | bytes 2359304 | tf_op jit(solution)/shard_map/ppermute | solution.py:54
  286.7 72.6 %collective-permute-start.21 = (bf16[528,768]{1,0:T(8,128)(2,1)S(1)}, bf16[528,768]{1,0:T(8,128)(2,1)S(1)}, u32[]{:S(2)}, u32[]{:S(2)}) collective-permute-start(bf16[528,768]{1,0:T(8,128)(2,1)S(1)} %copy-done.6), channel_id=1, source_target_pairs={{0,1},{3,2},{4,5},{7,6},{8,9},{11,10},{12,13},{15,14},{16,17},{19,... | collective-permute-start | bytes 2433032 | tf_op jit(solution)/shard_map/ppermute | solution.py:54
  288.0 49.5 %collective-permute-start.23 = (bf16[528,768]{1,0:T(8,128)(2,1)S(1)}, bf16[528,768]{1,0:T(8,128)(2,1)}, u32[]{:S(2)}, u32[]{:S(2)}) collective-permute-start(bf16[528,768]{1,0:T(8,128)(2,1)S(1)} %copy-done.8), channel_id=1, source_target_pairs={{0,1},{3,2},{4,5},{7,6},{8,9},{11,10},{12,13},{15,14},{16,17},{19,... | collective-permute-start | bytes 2433032 | tf_op jit(solution)/shard_map/ppermute | solution.py:54
  293.4 50.1 %collective-permute-start.61 = (bf16[384,768]{1,0:T(8,128)(2,1)}, bf16[384,768]{1,0:T(8,128)(2,1)}, u32[]{:S(2)}, u32[]{:S(2)}) collective-permute-start(bf16[384,768]{1,0:T(8,128)(2,1)} %constant_dynamic-slice_fusion.4), channel_id=1, source_target_pairs={{0,8},{4,12},{8,0},{12,4},{16,24},{20,28},{24,16},{28,20},{1,9},{5... | collective-permute-start | bytes 1769480 | tf_op jit(solution)/shard_map/ppermute | solution.py:58
  297.4 48.2 %collective-permute-start.67 = (bf16[384,768]{1,0:T(8,128)(2,1)}, bf16[384,768]{1,0:T(8,128)(2,1)}, u32[]{:S(2)}, u32[]{:S(2)}) collective-permute-start(bf16[384,768]{1,0:T(8,128)(2,1)} %constant_dynamic-slice_fusion.1), channel_id=1, source_target_pairs={{0,16},{4,20},{8,24},{12,28},{16,0},{20,4},{24,8},{28,12},{1,17},{... | collective-permute-start | bytes 1769480 | tf_op jit(solution)/shard_map/ppermute | solution.py:58
  337.5 22.9 %collective-permute-start.18 = (bf16[512,768]{1,0:T(8,128)(2,1)S(1)}, bf16[512,768]{1,0:T(8,128)(2,1)S(1)}, u32[]{:S(2)}, u32[]{:S(2)}) collective-permute-start(bf16[512,768]{1,0:T(8,128)(2,1)S(1)} %copy-done.18), channel_id=1, source_target_pairs={{0,1},{3,2},{4,5},{7,6},{8,9},{11,10},{12,13},{15,14},{16,17},{19,... | collective-permute-start | bytes 2359304 | tf_op jit(solution)/shard_map/ppermute | solution.py:54
  343.5 17.8 %collective-permute-start.24 = (bf16[528,768]{1,0:T(8,128)(2,1)S(1)}, bf16[528,768]{1,0:T(8,128)(2,1)S(1)}, u32[]{:S(2)}, u32[]{:S(2)}) collective-permute-start(bf16[528,768]{1,0:T(8,128)(2,1)S(1)} %add.416), channel_id=1, source_target_pairs={{1,2},{2,1},{5,6},{6,5},{9,10},{10,9},{13,14},{14,13},{17,18},{18,... | collective-permute-start | bytes 2433032 | tf_op jit(solution)/shard_map/ppermute | solution.py:54
  345.6 22.6 %collective-permute-start.62 = (bf16[192,768]{1,0:T(8,128)(2,1)S(1)}, bf16[192,768]{1,0:T(8,128)(2,1)S(1)}, u32[]{:S(2)}, u32[]{:S(2)}) collective-permute-start(bf16[192,768]{1,0:T(8,128)(2,1)S(1)} %constant_dynamic-slice_fusion.3), channel_id=1, source_target_pairs={{0,16},{4,20},{8,24},{12,28},{16,0},{20,4},{24,8},{28,12},{1,17},{... | collective-permute-start | bytes 884744 | tf_op jit(solution)/shard_map/ppermute | solution.py:58
  348.5 20.0 %collective-permute-start.68 = (bf16[192,768]{1,0:T(8,128)(2,1)S(1)}, bf16[192,768]{1,0:T(8,128)(2,1)S(1)}, u32[]{:S(2)}, u32[]{:S(2)}) collective-permute-start(bf16[192,768]{1,0:T(8,128)(2,1)S(1)} %constant_dynamic-slice_fusion), channel_id=1, source_target_pairs={{0,8},{4,12},{8,0},{12,4},{16,24},{20,28},{24,16},{28,20},{1,9},{5... | collective-permute-start | bytes 884744 | tf_op jit(solution)/shard_map/ppermute | solution.py:58
  359.5 21.8 %collective-permute-start.22 = (bf16[528,768]{1,0:T(8,128)(2,1)S(1)}, bf16[528,768]{1,0:T(8,128)(2,1)S(1)}, u32[]{:S(2)}, u32[]{:S(2)}) collective-permute-start(bf16[528,768]{1,0:T(8,128)(2,1)S(1)} %add.414), channel_id=1, source_target_pairs={{1,2},{2,1},{5,6},{6,5},{9,10},{10,9},{13,14},{14,13},{17,18},{18,... | collective-permute-start | bytes 2433032 | tf_op jit(solution)/shard_map/ppermute | solution.py:54
  360.6 16.5 %collective-permute-start.19 = (bf16[512,768]{1,0:T(8,128)(2,1)S(1)}, bf16[512,768]{1,0:T(8,128)(2,1)S(1)}, u32[]{:S(2)}, u32[]{:S(2)}) collective-permute-start(bf16[512,768]{1,0:T(8,128)(2,1)S(1)} %add.406), channel_id=1, source_target_pairs={{1,2},{2,1},{5,6},{6,5},{9,10},{10,9},{13,14},{14,13},{17,18},{18,... | collective-permute-start | bytes 2359304 | tf_op jit(solution)/shard_map/ppermute | solution.py:54
  361.5 43.5 %collective-permute-start.25 = (bf16[528,768]{1,0:T(8,128)(2,1)S(1)}, bf16[528,768]{1,0:T(8,128)(2,1)S(1)}, u32[]{:S(2)}, u32[]{:S(2)}) collective-permute-start(bf16[528,768]{1,0:T(8,128)(2,1)S(1)} %add.417), channel_id=1, source_target_pairs={{0,1},{1,0},{2,3},{3,2},{4,5},{5,4},{6,7},{7,6},{8,9},{9,8},{10,11... | collective-permute-start | bytes 2433032 | tf_op jit(solution)/shard_map/ppermute | solution.py:54
  368.3 9.8 %collective-permute-start.63 = (bf16[192,768]{1,0:T(8,128)(2,1)S(1)}, bf16[192,768]{1,0:T(8,128)(2,1)S(1)}, u32[]{:S(2)}, u32[]{:S(2)}) collective-permute-start(bf16[192,768]{1,0:T(8,128)(2,1)S(1)} %dynamic-slice_add_fusion.13), channel_id=1, source_target_pairs={{0,16},{4,20},{8,24},{12,28},{16,0},{20,4},{24,8},{28,12},{1,17},{... | collective-permute-start | bytes 884744 | tf_op jit(solution)/shard_map/ppermute | solution.py:58
  368.5 11.7 %collective-permute-start.69 = (bf16[192,768]{1,0:T(8,128)(2,1)S(1)}, bf16[192,768]{1,0:T(8,128)(2,1)S(1)}, u32[]{:S(2)}, u32[]{:S(2)}) collective-permute-start(bf16[192,768]{1,0:T(8,128)(2,1)S(1)} %dynamic-slice_add_fusion.12), channel_id=1, source_target_pairs={{0,8},{4,12},{8,0},{12,4},{16,24},{20,28},{24,16},{28,20},{1,9},{5... | collective-permute-start | bytes 884744 | tf_op jit(solution)/shard_map/ppermute | solution.py:58
  377.1 34.3 %collective-permute-start.13 = (bf16[512,768]{1,0:T(8,128)(2,1)S(1)}, bf16[512,768]{1,0:T(8,128)(2,1)S(1)}, u32[]{:S(2)}, u32[]{:S(2)}) collective-permute-start(bf16[512,768]{1,0:T(8,128)(2,1)S(1)} %add.404), channel_id=1, source_target_pairs={{1,2},{2,1},{5,6},{6,5},{9,10},{10,9},{13,14},{14,13},{17,18},{18,... | collective-permute-start | bytes 2359304 | tf_op jit(solution)/shard_map/ppermute | solution.py:54
  378.0 53.6 %collective-permute-start.48 = (bf16[1152,1024]{1,0:T(8,128)(2,1)}, bf16[1152,1024]{1,0:T(8,128)(2,1)}, u32[]{:S(2)}, u32[]{:S(2)}) collective-permute-start(bf16[1152,1024]{1,0:T(8,128)(2,1)} %constant_dynamic-slice_fusion.11), channel_id=1, source_target_pairs={{0,4},{4,0},{8,12},{12,8},{16,20},{20,16},{24,28},{28,24},{1,5},{5... | collective-permute-start | bytes 7077896 | tf_op jit(solution)/shard_map/ppermute | solution.py:58
  380.3 67.9 %collective-permute-start.54 = (bf16[1152,1024]{1,0:T(8,128)(2,1)}, bf16[1152,1024]{1,0:T(8,128)(2,1)S(1)}, u32[]{:S(2)}, u32[]{:S(2)}) collective-permute-start(bf16[1152,1024]{1,0:T(8,128)(2,1)} %constant_dynamic-slice_fusion.8), channel_id=1, source_target_pairs={{0,4},{4,0},{8,12},{12,8},{16,20},{20,16},{24,28},{28,24},{1,5},{5... | collective-permute-start | bytes 7077896 | tf_op jit(solution)/shard_map/ppermute | solution.py:58
  381.3 41.4 %collective-permute-start.20 = (bf16[512,768]{1,0:T(8,128)(2,1)S(1)}, bf16[512,768]{1,0:T(8,128)(2,1)S(1)}, u32[]{:S(2)}, u32[]{:S(2)}) collective-permute-start(bf16[512,768]{1,0:T(8,128)(2,1)S(1)} %add.407), channel_id=1, source_target_pairs={{0,1},{1,0},{2,3},{3,2},{4,5},{5,4},{6,7},{7,6},{8,9},{9,8},{10,11... | collective-permute-start | bytes 2359304 | tf_op jit(solution)/shard_map/ppermute | solution.py:54
  405.0 62.9 %collective-permute-start.64 = (bf16[384,768]{1,0:T(8,128)(2,1)}, bf16[384,768]{1,0:T(8,128)(2,1)}, u32[]{:S(2)}, u32[]{:S(2)}) collective-permute-start(bf16[384,768]{1,0:T(8,128)(2,1)} %maximum_select_fusion.14), channel_id=1, source_target_pairs={{0,8},{4,12},{8,0},{12,4},{16,24},{20,28},{24,16},{28,20},{1,9},{5... | collective-permute-start | bytes 1769480 | tf_op jit(solution)/shard_map/ppermute | solution.py:58
  411.4 59.6 %collective-permute-start.70 = (bf16[384,768]{1,0:T(8,128)(2,1)}, bf16[384,768]{1,0:T(8,128)(2,1)}, u32[]{:S(2)}, u32[]{:S(2)}) collective-permute-start(bf16[384,768]{1,0:T(8,128)(2,1)} %maximum_select_fusion.15), channel_id=1, source_target_pairs={{0,16},{4,20},{8,24},{12,28},{16,0},{20,4},{24,8},{28,12},{1,17},{... | collective-permute-start | bytes 1769480 | tf_op jit(solution)/shard_map/ppermute | solution.py:58
  435.2 5.2 collective-permute-start.44
  437.8 100.8 %collective-permute-start.49 = (bf16[576,1024]{1,0:T(8,128)(2,1)}, bf16[576,1024]{1,0:T(8,128)(2,1)}, u32[]{:S(2)}, u32[]{:S(2)}) collective-permute-start(bf16[576,1024]{1,0:T(8,128)(2,1)} %constant_dynamic-slice_fusion.10), channel_id=1, source_target_pairs={{0,8},{4,12},{8,0},{12,4},{16,24},{20,28},{24,16},{28,20},{1,9},{5... | collective-permute-start | bytes 3538952 | tf_op jit(solution)/shard_map/ppermute | solution.py:58
  440.4 10.6 %collective-permute-start.45 = (f32[28,768]{1,0:T(8,128)S(1)}, f32[28,768]{1,0:T(8,128)S(1)}, u32[]{:S(2)}, u32[]{:S(2)}) collective-permute-start(f32[28,768]{1,0:T(8,128)S(1)} %add.445), channel_id=1, source_target_pairs={{0,16},{4,20},{8,24},{12,28},{16,0},{20,4},{24,8},{28,12},{1,17},{... | collective-permute-start | bytes 258056 | tf_op jit(solution)/shard_map/ppermute | solution.py:58
  451.1 4.7 collective-permute-start.46
  454.0 86.9 %collective-permute-start.55 = (bf16[576,1024]{1,0:T(8,128)(2,1)}, bf16[576,1024]{1,0:T(8,128)(2,1)}, u32[]{:S(2)}, u32[]{:S(2)}) collective-permute-start(bf16[576,1024]{1,0:T(8,128)(2,1)} %constant_dynamic-slice_fusion.7), channel_id=1, source_target_pairs={{0,16},{4,20},{8,24},{12,28},{16,0},{20,4},{24,8},{28,12},{1,17},{... | collective-permute-start | bytes 3538952 | tf_op jit(solution)/shard_map/ppermute | solution.py:58
  455.8 5.7 collective-permute-start.47
  461.5 17.0 %collective-permute-start.26 = (bf16[512,768]{1,0:T(8,128)(2,1)S(1)}, bf16[512,768]{1,0:T(8,128)(2,1)S(1)}, u32[]{:S(2)}, u32[]{:S(2)}) collective-permute-start(bf16[512,768]{1,0:T(8,128)(2,1)S(1)} %copy-done.62), channel_id=1, source_target_pairs={{0,1},{1,0},{2,3},{3,2},{4,5},{5,4},{6,7},{7,6},{8,9},{9,8},{10,11... | collective-permute-start | bytes 2359304 | tf_op jit(solution)/shard_map/ppermute | solution.py:54
  471.0 182.8 %collective-permute-start.65 = (bf16[768,768]{1,0:T(8,128)(2,1)}, bf16[768,768]{1,0:T(8,128)(2,1)}, u32[]{:S(2)}, u32[]{:S(2)}) collective-permute-start(bf16[768,768]{1,0:T(8,128)(2,1)} %maximum_select_fusion.10), channel_id=1, source_target_pairs={{0,4},{4,0},{8,12},{12,8},{16,20},{20,16},{24,28},{28,24},{1,5},{5... | collective-permute-start | bytes 3538952 | tf_op jit(solution)/shard_map/ppermute | solution.py:58
  474.2 189.6 %collective-permute-start.71 = (bf16[768,768]{1,0:T(8,128)(2,1)}, bf16[768,768]{1,0:T(8,128)(2,1)}, u32[]{:S(2)}, u32[]{:S(2)}) collective-permute-start(bf16[768,768]{1,0:T(8,128)(2,1)} %maximum_select_fusion.11), channel_id=1, source_target_pairs={{0,4},{4,0},{8,12},{12,8},{16,20},{20,16},{24,28},{28,24},{1,5},{5... | collective-permute-start | bytes 3538952 | tf_op jit(solution)/shard_map/ppermute | solution.py:58
  536.4 16.3 %collective-permute-start.33 = (bf16[384,768]{1,0:T(8,128)(2,1)S(1)}, bf16[384,768]{1,0:T(8,128)(2,1)S(1)}, u32[]{:S(2)}, u32[]{:S(2)}) collective-permute-start(bf16[384,768]{1,0:T(8,128)(2,1)S(1)} %constant_dynamic-slice_fusion.17), channel_id=1, source_target_pairs={{0,16},{4,20},{8,24},{12,28},{16,0},{20,4},{24,8},{28,12},{1,17},{... | collective-permute-start | bytes 1769480 | tf_op jit(solution)/shard_map/ppermute | solution.py:58
  538.6 26.7 %collective-permute-start.36 = (bf16[384,768]{1,0:T(8,128)(2,1)S(1)}, bf16[384,768]{1,0:T(8,128)(2,1)S(1)}, u32[]{:S(2)}, u32[]{:S(2)}) collective-permute-start(bf16[384,768]{1,0:T(8,128)(2,1)S(1)} %constant_dynamic-slice_fusion.14), channel_id=1, source_target_pairs={{0,16},{4,20},{8,24},{12,28},{16,0},{20,4},{24,8},{28,12},{1,17},{... | collective-permute-start | bytes 1769480 | tf_op jit(solution)/shard_map/ppermute | solution.py:58
  540.9 35.9 %collective-permute-start.27 = (bf16[512,768]{1,0:T(8,128)(2,1)S(1)}, bf16[512,768]{1,0:T(8,128)(2,1)S(1)}, u32[]{:S(2)}, u32[]{:S(2)}) collective-permute-start(bf16[512,768]{1,0:T(8,128)(2,1)S(1)} %get-tuple-element.80), channel_id=1, source_target_pairs={{0,1},{1,0},{2,3},{3,2},{4,5},{5,4},{6,7},{7,6},{8,9},{9,8},{10,11... | collective-permute-start | bytes 2359304 | tf_op jit(solution)/shard_map/ppermute | solution.py:54
  552.7 22.0 %collective-permute-start.50 = (bf16[288,1024]{1,0:T(8,128)(2,1)S(1)}, bf16[288,1024]{1,0:T(8,128)(2,1)S(1)}, u32[]{:S(2)}, u32[]{:S(2)}) collective-permute-start(bf16[288,1024]{1,0:T(8,128)(2,1)S(1)} %constant_dynamic-slice_fusion.9), channel_id=1, source_target_pairs={{0,16},{4,20},{8,24},{12,28},{16,0},{20,4},{24,8},{28,12},{1,17},{... | collective-permute-start | bytes 1769480 | tf_op jit(solution)/shard_map/ppermute | solution.py:58
  565.3 14.0 %collective-permute-start.56 = (bf16[288,1024]{1,0:T(8,128)(2,1)S(1)}, bf16[288,1024]{1,0:T(8,128)(2,1)S(1)}, u32[]{:S(2)}, u32[]{:S(2)}) collective-permute-start(bf16[288,1024]{1,0:T(8,128)(2,1)S(1)} %constant_dynamic-slice_fusion.6), channel_id=1, source_target_pairs={{0,8},{4,12},{8,0},{12,4},{16,24},{20,28},{24,16},{28,20},{1,9},{5... | collective-permute-start | bytes 1769480 | tf_op jit(solution)/shard_map/ppermute | solution.py:58
  575.0 10.3 %collective-permute-start.51 = (bf16[288,1024]{1,0:T(8,128)(2,1)S(1)}, bf16[288,1024]{1,0:T(8,128)(2,1)S(1)}, u32[]{:S(2)}, u32[]{:S(2)}) collective-permute-start(bf16[288,1024]{1,0:T(8,128)(2,1)S(1)} %dynamic-slice_add_fusion.9), channel_id=1, source_target_pairs={{0,16},{4,20},{8,24},{12,28},{16,0},{20,4},{24,8},{28,12},{1,17},{... | collective-permute-start | bytes 1769480 | tf_op jit(solution)/shard_map/ppermute | solution.py:58
  576.8 10.9 %collective-permute-start.37 = (bf16[192,768]{1,0:T(8,128)(2,1)S(1)}, bf16[192,768]{1,0:T(8,128)(2,1)S(1)}, u32[]{:S(2)}, u32[]{:S(2)}) collective-permute-start(bf16[192,768]{1,0:T(8,128)(2,1)S(1)} %constant_dynamic-slice_fusion.13), channel_id=1, source_target_pairs={{0,8},{4,12},{8,0},{12,4},{16,24},{20,28},{24,16},{28,20},{1,9},{5... | collective-permute-start | bytes 884744 | tf_op jit(solution)/shard_map/ppermute | solution.py:58
  579.6 19.9 %collective-permute-start.57 = (bf16[288,1024]{1,0:T(8,128)(2,1)S(1)}, bf16[288,1024]{1,0:T(8,128)(2,1)S(1)}, u32[]{:S(2)}, u32[]{:S(2)}) collective-permute-start(bf16[288,1024]{1,0:T(8,128)(2,1)S(1)} %dynamic-slice_add_fusion.8), channel_id=1, source_target_pairs={{0,8},{4,12},{8,0},{12,4},{16,24},{20,28},{24,16},{28,20},{1,9},{5... | collective-permute-start | bytes 1769480 | tf_op jit(solution)/shard_map/ppermute | solution.py:58
  585.9 41.8 %collective-permute-start.52 = (bf16[576,1024]{1,0:T(8,128)(2,1)S(1)}, bf16[576,1024]{1,0:T(8,128)(2,1)S(1)}, u32[]{:S(2)}, u32[]{:S(2)}) collective-permute-start(bf16[576,1024]{1,0:T(8,128)(2,1)S(1)} %maximum_select_fusion.8), channel_id=1, source_target_pairs={{0,8},{4,12},{8,0},{12,4},{16,24},{20,28},{24,16},{28,20},{1,9},{5... | collective-permute-start | bytes 3538952 | tf_op jit(solution)/shard_map/ppermute | solution.py:58
  587.7 38.1 %collective-permute-start.34 = (bf16[192,768]{1,0:T(8,128)(2,1)S(1)}, bf16[192,768]{1,0:T(8,128)(2,1)S(1)}, u32[]{:S(2)}, u32[]{:S(2)}) collective-permute-start(bf16[192,768]{1,0:T(8,128)(2,1)S(1)} %constant_dynamic-slice_fusion.16), channel_id=1, source_target_pairs={{0,8},{4,12},{8,0},{12,4},{16,24},{20,28},{24,16},{28,20},{1,9},{5... | collective-permute-start | bytes 884744 | tf_op jit(solution)/shard_map/ppermute | solution.py:58
  599.5 28.0 %collective-permute-start.38 = (bf16[96,768]{1,0:T(8,128)(2,1)S(1)}, bf16[96,768]{1,0:T(8,128)(2,1)S(1)}, u32[]{:S(2)}, u32[]{:S(2)}) collective-permute-start(bf16[96,768]{1,0:T(8,128)(2,1)S(1)} %constant_dynamic-slice_fusion.12), channel_id=1, source_target_pairs={{0,4},{4,0},{8,12},{12,8},{16,20},{20,16},{24,28},{28,24},{1,5},{5... | collective-permute-start | bytes 442376 | tf_op jit(solution)/shard_map/ppermute | solution.py:58
  625.8 23.4 %collective-permute-start.58 = (bf16[576,1024]{1,0:T(8,128)(2,1)S(1)}, bf16[576,1024]{1,0:T(8,128)(2,1)S(1)}, u32[]{:S(2)}, u32[]{:S(2)}) collective-permute-start(bf16[576,1024]{1,0:T(8,128)(2,1)S(1)} %maximum_select_fusion.9), channel_id=1, source_target_pairs={{0,16},{4,20},{8,24},{12,28},{16,0},{20,4},{24,8},{28,12},{1,17},{... | collective-permute-start | bytes 3538952 | tf_op jit(solution)/shard_map/ppermute | solution.py:58
  627.6 10.4 %collective-permute-start.39 = (bf16[96,768]{1,0:T(8,128)(2,1)S(1)}, bf16[96,768]{1,0:T(8,128)(2,1)S(1)}, u32[]{:S(2)}, u32[]{:S(2)}) collective-permute-start(bf16[96,768]{1,0:T(8,128)(2,1)S(1)} %dynamic-slice_add_fusion.16), channel_id=1, source_target_pairs={{0,2},{1,3},{2,0},{3,1},{4,6},{5,7},{6,4},{7,5},{8,10},{9,11},{10,... | collective-permute-start | bytes 442376 | tf_op jit(solution)/shard_map/ppermute | solution.py:54
  630.7 48.6 %collective-permute-start.53 = (bf16[1152,1024]{1,0:T(8,128)(2,1)S(1)}, bf16[1152,1024]{1,0:T(8,128)(2,1)S(1)}, u32[]{:S(2)}, u32[]{:S(2)}) collective-permute-start(bf16[1152,1024]{1,0:T(8,128)(2,1)S(1)} %maximum_select_fusion.2), channel_id=1, source_target_pairs={{0,4},{4,0},{8,12},{12,8},{16,20},{20,16},{24,28},{28,24},{1,5},{5... | collective-permute-start | bytes 7077896 | tf_op jit(solution)/shard_map/ppermute | solution.py:58
  638.1 14.2 %collective-permute-start.40 = (bf16[96,768]{1,0:T(8,128)(2,1)S(1)}, bf16[96,768]{1,0:T(8,128)(2,1)S(1)}, u32[]{:S(2)}, u32[]{:S(2)}) collective-permute-start(bf16[96,768]{1,0:T(8,128)(2,1)S(1)} %add_add_fusion.1), channel_id=1, source_target_pairs={{0,4},{4,0},{8,12},{12,8},{16,20},{20,16},{24,28},{28,24},{1,5},{5... | collective-permute-start | bytes 442376 | tf_op jit(solution)/shard_map/ppermute | solution.py:58
  650.5 31.5 %collective-permute-start.59 = (bf16[1152,1024]{1,0:T(8,128)(2,1)S(1)}, bf16[1152,1024]{1,0:T(8,128)(2,1)S(1)}, u32[]{:S(2)}, u32[]{:S(2)}) collective-permute-start(bf16[1152,1024]{1,0:T(8,128)(2,1)S(1)} %maximum_select_fusion.3), channel_id=1, source_target_pairs={{0,4},{4,0},{8,12},{12,8},{16,20},{20,16},{24,28},{28,24},{1,5},{5... | collective-permute-start | bytes 7077896 | tf_op jit(solution)/shard_map/ppermute | solution.py:58
  652.3 9.5 %collective-permute-start.41 = (bf16[192,768]{1,0:T(8,128)(2,1)S(1)}, bf16[192,768]{1,0:T(8,128)(2,1)S(1)}, u32[]{:S(2)}, u32[]{:S(2)}) collective-permute-start(bf16[192,768]{1,0:T(8,128)(2,1)S(1)} %maximum_select_fusion.17), channel_id=1, source_target_pairs={{0,8},{4,12},{8,0},{12,4},{16,24},{20,28},{24,16},{28,20},{1,9},{5... | collective-permute-start | bytes 884744 | tf_op jit(solution)/shard_map/ppermute | solution.py:58
  662.0 15.0 %collective-permute-start.42 = (bf16[384,768]{1,0:T(8,128)(2,1)S(1)}, bf16[384,768]{1,0:T(8,128)(2,1)S(1)}, u32[]{:S(2)}, u32[]{:S(2)}) collective-permute-start(bf16[384,768]{1,0:T(8,128)(2,1)S(1)} %maximum_select_fusion.13), channel_id=1, source_target_pairs={{0,16},{4,20},{8,24},{12,28},{16,0},{20,4},{24,8},{28,12},{1,17},{... | collective-permute-start | bytes 1769480 | tf_op jit(solution)/shard_map/ppermute | solution.py:58
  (94 other events, 765.9 us)
